TPU v7x, 32 devices: a whole 2x2x4 slice. The times are simulated.
32 devices in a mesh: dp: 4 (over y, core), table: 8 (over z, x).
Axes of the slice: x: 2, y: 2, z: 4, core: 2. Of those that a mesh axis runs over, the one named last changes fastest.
Arguments:
- embedded: bfloat16 [2, 2048, 4096], P(None, 'dp', 'table'), may hold values from -1.1953125 to 1.1953125
- resid_grad: bfloat16 [2, 2048, 4096], P(None, 'dp', 'table'), may hold values from -0.29882812 to 0.29882812
- query_grad: bfloat16 [2, 2048, 2048], P(None, ('dp', 'table')), may hold values from -0.59765625 to 0.59765625
- query_weight: bfloat16 [4096, 2048], P('table'), may hold values from -0.09375 to 0.09375
- ngram_rows: int32 [2, 2048, 4], P(None, 'dp'), may hold values from 0 to 799999, as said below
- touched_rows: int32 [8, 4, 12], replicated, may hold values from -1 to 799999, as said below
- row_values: float32 [8, 4, 12, 1024], P('table'), may hold values from -6 to 6
- row_mean: float32 [8, 4, 12, 1024], P('table'), may hold values from -0.6 to 0.6
- row_square: float32 [8, 4, 12, 1024], P('table'), may hold values from 0.01 to 0.1
Outputs:
- weight_grad: float32 [4096, 2048], P('table')
- new_values: float32 [8, 4, 12, 1024], P('table')
- new_mean: float32 [8, 4, 12, 1024], P('table')
- new_square: float32 [8, 4, 12, 1024], P('table')
Inputs may be any that keep to these rules, and one draw needn't show every extreme that they name: `touched_rows`: owner o's list for slice s holds 1 to 12 distinct row ids of [o * 100000, (o + 1) * 100000) first, then -1; in every slice some owner's list is full. `ngram_rows`: every id of slice s is one of the listed rows of owner id // 100000 for slice s.
All inputs are finite; a program needn't handle non-finite values.
Results may differ from a plain program's by a relative error of at most 0.0003.
Values may be sent and summed in bfloat16 or wider, within the bound.
A program may use at most 64 MiB of HBM per device.

v0:
```python
import jax
import jax.numpy as jnp
from jax import lax
from jax.sharding import PartitionSpec as P

SLICES = 4
SW = 1024


beta_one = 0.9
beta_two = 0.95
learn_rate = 0.01
adam_eps = 1e-08
adam_step = 10


def adam_rows(grads, values, mean, square, live):
    corr_one = 1.0 - beta_one**adam_step
    corr_two = 1.0 - beta_two**adam_step
    mean_next = beta_one * mean + (1.0 - beta_one) * grads
    square_next = beta_two * square + (1.0 - beta_two) * grads * grads
    update = learn_rate * (mean_next / corr_one) / (jnp.sqrt(square_next / corr_two) + adam_eps)
    values_next = values - update
    return (
        jnp.where(live, values_next, values),
        jnp.where(live, mean_next, mean),
        jnp.where(live, square_next, square),
    )


def make_step(emb_part, weight_part, carry, piece):
    back_part, wgrad = carry
    back = jnp.einsum("mrh,ph->mrp", piece, weight_part, preferred_element_type=jnp.float32)
    back_part = back
    wgrad = wgrad + jnp.einsum("mrp,mrh->ph", emb_part, piece, preferred_element_type=jnp.float32)
    return (back_part, wgrad)


def local(
    embedded,
    resid_grad,
    query_grad,
    query_weight,
    ngram_rows,
    touched_rows,
    row_values,
    row_mean,
    row_square,
):
    micro_count, group_tokens, width_part = embedded.shape
    hidden = query_grad.shape[2]
    tables = lax.axis_size("table")
    table_idx = lax.axis_index("table")
    zero_grad = jnp.zeros((width_part, hidden), jnp.float32)
    wgrad = zero_grad
    backs = []
    for micro in range(micro_count):
        start_back = jnp.zeros((1, group_tokens, width_part), jnp.float32)
        back_one, wgrad = make_step(
            embedded[micro : micro + 1],
            query_weight,
            (start_back, wgrad),
            lax.all_gather(query_grad[micro : micro + 1], "table", axis=1, tiled=True),
        )
        backs.append(back_one)
    back_all = jnp.concatenate(backs, axis=0)
    emb_grad = resid_grad.astype(jnp.float32) + back_all
    weight_grad = lax.psum(wgrad, "dp")
    slice_idx = table_idx * width_part // SW
    ids = lax.dynamic_index_in_dim(ngram_rows, slice_idx, 2, False)
    listed = lax.dynamic_index_in_dim(touched_rows, slice_idx, 1, False)
    entries = listed.shape[1]
    flat_list = listed.reshape(tables * entries)
    onehot = (ids[:, :, None] == flat_list[None, None, :]).astype(jnp.float32)
    buckets = jnp.einsum(
        "mtk,mtp->kp",
        onehot,
        emb_grad,
        precision=lax.Precision.HIGHEST,
        preferred_element_type=jnp.float32,
    )
    buckets = buckets.reshape(tables, entries, width_part)
    arrived = lax.all_to_all(buckets, "table", split_axis=0, concat_axis=0, tiled=True)
    per_slice = tables // SLICES
    local_grad = (
        arrived.reshape(SLICES, per_slice, entries, width_part)
        .transpose(0, 2, 1, 3)
        .reshape(SLICES, entries, per_slice * width_part)
    )
    mine = lax.dynamic_index_in_dim(touched_rows, table_idx, 0, False)
    live = (mine >= 0)[..., None]
    values = row_values[0]
    mean = row_mean[0]
    square = row_square[0]
    grads = lax.psum(local_grad, "dp")
    values_next, mean_next, square_next = adam_rows(grads, values, mean, square, live)
    return (weight_grad, values_next[None], mean_next[None], square_next[None])


def solution(mesh):
    placed = (
        P(None, "dp", "table"),
        P(None, "dp", "table"),
        P(None, ("dp", "table"), None),
        P("table", None),
        P(None, "dp", None),
        P(),
        P("table", None, None, None),
        P("table", None, None, None),
        P("table", None, None, None),
    )
    return jax.shard_map(
        local,
        mesh=mesh,
        in_specs=placed,
        out_specs=(
            P("table", None),
            P("table", None, None, None),
            P("table", None, None, None),
            P("table", None, None, None),
        ),
        check_vma=False,
    )
```

profile of v0, /device:TPU:0, one launch (start us, length us, event | category | flops | bytes accessed | tf_op | source)
XLA Modules:
  0.0 232.1 jit_solution(5300985283279958009)
XLA Ops:
  7.2 0.0 copy-start
  7.2 0.0 all-gather.3.cloned.1.call-start
  7.2 2.0 fusion.32
  9.2 0.0 all-gather.3.cloned.1.call-update
  9.3 0.0 all-gather.5.cloned.1.call-start
  9.3 0.7 all-gather.5.cloned.1.call-update
  10.0 0.7 constant_dynamic-slice_fusion
  10.8 0.7 dynamic-slice_reduce_fusion
  11.5 0.1 eq.19
  11.6 51.1 %all-gather.3.cloned.1.call-done = bf16[1,512,2048]{2,1,0:T(8,128)(2,1)} async-done(((bf16[1,64,2048]{2,1,0:T(8,128)(2,1)}), bf16[1,512,2048]{2,1,0:T(8,128)(2,1)}) %all-gather.3.cloned.1.call-update) | async-done | bytes 2097168 | tf_op jit(solution)/shard_map/all_gather | solution.py:63
  62.7 0.0 copy-done
  62.7 3.8 %fusion.11 = f32[1,512,512]{2,1,0:T(8,128)} fusion(bf16[512,2048]{1,0:T(8,128)(2,1)S(1)} %copy-done, bf16[1,512,2048]{2,1,0:T(8,128)(2,1)} %all-gather.3.cloned.1.call-done), kind=kOutput, calls=%fused_computation.13 | convolution fusion | flops 1073741824 | bytes 5242880 | tf_op jit(solution)/shard_map/mrh,ph->mrp/dot_general | solution.py:33
  66.6 46.1 %all-gather.5.cloned.1.call-done = bf16[1,512,2048]{2,1,0:T(8,128)(2,1)} async-done(((bf16[1,64,2048]{2,1,0:T(8,128)(2,1)}), bf16[1,512,2048]{2,1,0:T(8,128)(2,1)}) %all-gather.5.cloned.1.call-update) | async-done | bytes 2097168 | tf_op jit(solution)/shard_map/all_gather | solution.py:63
  112.7 0.0 copy-start.3
  112.7 0.0 copy-start.4
  112.7 3.0 %fusion.14 = f32[1,512,512]{2,1,0:T(8,128)S(1)} fusion(bf16[512,2048]{1,0:T(8,128)(2,1)S(1)} %copy-done, bf16[1,512,2048]{2,1,0:T(8,128)(2,1)} %all-gather.5.cloned.1.call-done), kind=kOutput, calls=%fused_computation.14 | convolution fusion | flops 1073741824 | bytes 5242880 | tf_op jit(solution)/shard_map/mrh,ph->mrp/dot_general | solution.py:33
  115.7 0.0 copy-done.3
  115.7 0.0 copy-done.4
  115.7 0.0 copy-start.2
  115.7 1.0 fusion.17
  116.8 0.7 reshape.46
  117.5 3.4 %all-to-all-start = ((f32[8,12,512]{2,1,0:T(8,128)}), f32[8,12,512]{2,1,0:T(8,128)S(1)}, u32[]{:S(2)}, u32[]{:S(2)}) async-start(f32[8,12,512]{2,1,0:T(8,128)} %reshape.46), calls=%async_computation | async-start | bytes 524288 | tf_op jit(solution)/shard_map/all_to_all | solution.py:83
  120.9 0.0 all-reduce.3.cloned.1.call-start
  121.0 0.0 copy-done.2
  121.0 0.0 copy-start.1
  121.0 3.0 %fusion.8 = f32[512,2048]{1,0:T(8,128)S(1)} fusion(bf16[1,512,2048]{2,1,0:T(8,128)(2,1)} %all-gather.3.cloned.1.call-done, bf16[2,512,512]{2,1,0:T(8,128)(2,1)S(1)} %copy-done.2), kind=kOutput, calls=%fused_computation.10 | convolution fusion | flops 1073741824 | bytes 6815744 | tf_op jit(solution)/shard_map/mrp,mrh->ph/dot_general | solution.py:35
  124.0 0.0 copy-done.1
  124.0 3.4 %convolution_add_fusion = f32[512,2048]{1,0:T(8,128)} fusion(f32[512,2048]{1,0:T(8,128)S(1)} %fusion.8, bf16[1,512,2048]{2,1,0:T(8,128)(2,1)S(1)} %copy-done.1, bf16[2,512,512]{2,1,0:T(8,128)(2,1)S(1)} %copy-done.2), kind=kOutput, calls=%fused_computation | convolution fusion | flops 1074790400 | bytes 11010048 | tf_op jit(solution)/shard_map/mrp,mrh->ph/dot_general | solution.py:35
  127.4 2.1 all-to-all-done
  129.4 0.2 copy.16
  129.6 0.9 reshape.48
  130.5 0.0 copy-start.5
  130.5 0.0 copy-start.6
  130.5 0.0 copy-start.7
  130.5 0.0 all-reduce.3.cloned.1.call-update
  130.5 0.8 fusion.30
  131.3 0.1 copy.15
  131.4 87.4 %all-reduce.3.cloned.1.call-done = (f32[512,2048]{1,0:T(8,128)}, f32[4,12,1024]{2,0,1:T(4,128)}) async-done(((f32[512,2048]{1,0:T(8,128)}, f32[4,12,1024]{2,0,1:T(4,128)}), (f32[512,2048]{1,0:T(8,128)}, f32[4,12,1024]{2,0,1:T(4,128)})) %all-reduce.3.cloned.1.call-update) | async-done | bytes 4390928 | tf_op jit(solution)/shard_map/psum | solution.py:68
  218.8 0.0 copy-done.5
  218.8 0.0 copy-done.6
  218.8 0.0 copy-done.7
  218.8 2.1 fusion.25
  220.9 4.7 %copy.22 = f32[512,2048]{1,0:T(8,128)} copy(f32[512,2048]{1,0:T(8,128)} %get-tuple-element.11) | data formatting | bytes 8388608
  (1 shorter events, 0.0 us)
Async XLA Ops:
  7.2 55.6 %copy-start = (bf16[512,2048]{1,0:T(8,128)(2,1)S(1)}, bf16[512,2048]{1,0:T(8,128)(2,1)}, u32[]{:S(2)}) copy-start(bf16[512,2048]{1,0:T(8,128)(2,1)} %param.12) | copy-start | bytes 6291460
  7.2 55.6 %all-gather.3.cloned.1.call-start = ((), (), s32[]{:S(2)}) async-start(), calls=%async_computation.1 | async-start | bytes 2359296 | tf_op jit(solution)/shard_map/all_gather | solution.py:63
  9.3 103.4 %all-gather.5.cloned.1.call-start = ((), (), s32[]{:S(2)}) async-start(), calls=%async_computation.2 | async-start | bytes 2359296 | tf_op jit(solution)/shard_map/all_gather | solution.py:63
  112.7 3.0 %copy-start.3 = (bf16[2,512,512]{2,1,0:T(8,128)(2,1)S(1)}, bf16[2,512,512]{2,1,0:T(8,128)(2,1)}, u32[]{:S(2)}) copy-start(bf16[2,512,512]{2,1,0:T(8,128)(2,1)} %param.10) | copy-start | bytes 3145732
  112.7 3.0 %copy-start.4 = (f32[1,512,512]{2,1,0:T(8,128)S(1)}, f32[1,512,512]{2,1,0:T(8,128)}, u32[]{:S(2)}) copy-start(f32[1,512,512]{2,1,0:T(8,128)} %fusion.11) | copy-start | bytes 3145732
  115.7 5.3 %copy-start.2 = (bf16[2,512,512]{2,1,0:T(8,128)(2,1)S(1)}, bf16[2,512,512]{2,1,0:T(8,128)(2,1)}, u32[]{:S(2)}) copy-start(bf16[2,512,512]{2,1,0:T(8,128)(2,1)} %param.9) | copy-start | bytes 3145732
  117.5 11.9 %all-to-all-start = ((f32[8,12,512]{2,1,0:T(8,128)}), f32[8,12,512]{2,1,0:T(8,128)S(1)}, u32[]{:S(2)}, u32[]{:S(2)}) async-start(f32[8,12,512]{2,1,0:T(8,128)} %reshape.46), calls=%async_computation | async-start | bytes 524288 | tf_op jit(solution)/shard_map/all_to_all | solution.py:83
  120.9 97.8 %all-reduce.3.cloned.1.call-start = ((), (), s32[]{:S(2)}) async-start(), calls=%async_computation.3 | async-start | bytes 8781824 | tf_op jit(solution)/shard_map/psum | solution.py:68
  121.0 3.0 %copy-start.1 = (bf16[1,512,2048]{2,1,0:T(8,128)(2,1)S(1)}, bf16[1,512,2048]{2,1,0:T(8,128)(2,1)}, u32[]{:S(2)}) copy-start(bf16[1,512,2048]{2,1,0:T(8,128)(2,1)} %all-gather.5.cloned.1.call-done) | copy-start | bytes 6291460
  130.5 88.3 %copy-start.5 = (f32[1,4,12,1024]{3,1,2,0:T(4,128)S(1)}, f32[1,4,12,1024]{3,1,2,0:T(4,128)}, u32[]{:S(2)}) copy-start(f32[1,4,12,1024]{3,1,2,0:T(4,128)} %param.17) | copy-start | bytes 589828
  130.5 88.3 %copy-start.6 = (f32[1,4,12,1024]{3,1,2,0:T(4,128)S(1)}, f32[1,4,12,1024]{3,1,2,0:T(4,128)}, u32[]{:S(2)}) copy-start(f32[1,4,12,1024]{3,1,2,0:T(4,128)} %param.16) | copy-start | bytes 589828
  130.5 88.3 %copy-start.7 = (f32[1,4,12,1024]{3,1,2,0:T(4,128)S(1)}, f32[1,4,12,1024]{3,1,2,0:T(4,128)}, u32[]{:S(2)}) copy-start(f32[1,4,12,1024]{3,1,2,0:T(4,128)} %param.15) | copy-start | bytes 589828
Sparse Core Ops, SparseCore 0:
  10.7 51.9 all-gather.2
  64.9 47.7 all-gather.4
  130.6 88.0 all-reduce.2
where the time goes:
time: 233 us; the launch traced here: 232 us
  waiting for transfers between devices  187 us (80%)
  matrix products  14.3 us (6%)
  between operations  13.9 us (6%)
  local copies, waits for them, and re-layouts  10.2 us (4%)
  starting transfers between devices  3.53 us (2%)
  other arithmetic  2.89 us (1%)
    all_gather x2, waiting for transfers between devices, local(): lax.all_gather(query_grad[micro:micro + 1], 'table', axis=1, tiled=True)  97.2 us
    psum x1, waiting for transfers between devices, local(): weight_grad = lax.psum(wgrad, 'dp')  87.4 us
    dot_general x2, matrix products, make_step(): jnp.einsum('mrh,ph->mrp', piece, weight_part, preferred_element_type=jnp....  6.86 us
    dot_general x2, matrix products, make_step(): jnp.einsum('mrp,mrh->ph', emb_part, piece, preferred_element_type=jnp.flo...  6.39 us
    unnamed x18, local copies, waits for them, and re-layouts  4.74 us
  transfers between devices with their start and end apart: 4, of which 4 were waited for; matrix products, arithmetic and copies ran while one was open for 5% of the time, Pallas kernels for 0%

commit v1 on v0

--- a/solution.py
+++ b/solution.py
@@ -1,6 +1,10 @@
+import functools
+
 import jax
 import jax.numpy as jnp
 from jax import lax
+from jax.experimental import pallas as pl
+from jax.experimental.pallas import tpu as pltpu
 from jax.sharding import PartitionSpec as P
 
 SLICES = 4
@@ -97,6 +101,443 @@
     return (weight_grad, values_next[None], mean_next[None], square_next[None])
 
 
+CHUNKS = 8
+SLOT = 16
+MESH = pl.DeviceIdType.MESH
+UP, DOWN, ACROSS = 0, 1, 2
+
+
+def kernel(
+    emb_hbm,
+    resid_hbm,
+    qg_hbm,
+    w_hbm,
+    onehot,
+    out_hbm,
+    grads_out,
+    emb,
+    emb_t,
+    resid,
+    w,
+    gq,
+    part_own,
+    part_send,
+    part_recv,
+    q_send,
+    q_recv,
+    s_send,
+    s_recv,
+    res,
+    bucket,
+    b_send,
+    b_recv,
+    y_send,
+    y_recv,
+    a_send,
+    a_recv,
+    sib_recv,
+    load_sem,
+    g_send_sem,
+    g_recv_sem,
+    p_sem,
+    q_sem,
+    s_sem,
+    f_sem,
+    o_sem,
+    b_sem,
+    y_sem,
+    a_send_sem,
+    a_recv_sem,
+    h_sem,
+):
+    dp, me = lax.axis_index("dp"), lax.axis_index("table")
+    y, core = dp // 2, dp % 2
+    z, x = me // 2, me % 2
+    sib = dp + 1 - 2 * core
+    ynb = (1 - y) * 2 + core
+    zpair = z + 1 - 2 * (z % 2)
+    micro, mine, hidden = qg_hbm.shape
+    cols = hidden // CHUNKS
+    rows = emb_t.shape[0] // 2
+
+    barrier = pltpu.get_barrier_semaphore()
+    for step in range(1, 8):
+        pl.semaphore_signal(barrier, inc=1, device_id=(dp, (me + step) % 8), device_id_type=MESH)
+    pl.semaphore_signal(barrier, inc=1, device_id=(sib, me), device_id_type=MESH)
+    pl.semaphore_signal(barrier, inc=1, device_id=(ynb, me), device_id_type=MESH)
+
+    loads = [
+        pltpu.make_async_copy(emb_hbm, emb, load_sem.at[0]),
+        pltpu.make_async_copy(resid_hbm, resid, load_sem.at[1]),
+        pltpu.make_async_copy(w_hbm, w, load_sem.at[2]),
+    ]
+    for load in loads:
+        load.start()
+
+    def span(c):
+        return pl.ds(pl.multiple_of(c * cols, cols), cols)
+
+    def tokens(t):
+        return pl.ds(pl.multiple_of(t * mine, mine), mine)
+
+    def held(c, t):
+        return gq.at[c, :, tokens(t), :]
+
+    def own_load(c):
+        return pltpu.make_async_copy(qg_hbm.at[:, :, span(c)], held(c, me), load_sem.at[3 + c])
+
+    for c in range(CHUNKS):
+        own_load(c).start()
+
+    pl.semaphore_wait(barrier, 9)
+
+    def shard_copy(c, t, way, source=None):
+        to_z = z + 1 if way == UP else z - 1
+        to = (dp, to_z * 2 + x) if way != ACROSS else (dp, z * 2 + 1 - x)
+        return pltpu.make_async_remote_copy(
+            src_ref=held(c, t) if source is None else source,
+            dst_ref=held(c, t),
+            send_sem=g_send_sem.at[c, t, way],
+            recv_sem=g_recv_sem.at[c, t],
+            device_id=to,
+            device_id_type=MESH,
+        )
+
+    def arrived(c, t):
+        shard_copy(c, t, ACROSS).wait_recv()
+
+    def each_own(c, act):
+        own = qg_hbm.at[:, :, span(c)]
+
+        @pl.when(z < 3)
+        def _():
+            act(shard_copy(c, me, UP, own))
+
+        @pl.when(z > 0)
+        def _():
+            act(shard_copy(c, me, DOWN, own))
+
+        act(shard_copy(c, me, ACROSS, own))
+
+    def each_forward(c, far, act, wait):
+        for sign, way in ((-1, UP), (1, DOWN)):
+            from_z = z + sign * far
+            t = from_z * 2 + x
+            there = from_z >= 0 if sign < 0 else from_z < 4
+            onward = z < 3 if way == UP else z > 0
+
+            @pl.when(there)
+            def _():
+                if wait:
+                    arrived(c, t)
+
+                @pl.when(onward)
+                def _():
+                    act(shard_copy(c, t, way))
+
+                if far == 1:
+
+                    @pl.when((c % 2 == 0) | (from_z != zpair))
+                    def _():
+                        act(shard_copy(c, t, ACROSS))
+                else:
+                    act(shard_copy(c, t, ACROSS))
+
+    def each_relay(c, act, wait):
+        t = z * 2 + 1 - x
+
+        @pl.when(c % 2 == 1)
+        def _():
+            if wait:
+                arrived(c, t)
+
+            @pl.when(z % 2 == 0)
+            def _():
+                act(shard_copy(c, t, UP))
+
+            @pl.when(z % 2 == 1)
+            def _():
+                act(shard_copy(c, t, DOWN))
+
+    def start(copy):
+        copy.start()
+
+    def sibling_copy(src, dst, sems):
+        return pltpu.make_async_remote_copy(
+            src_ref=src, dst_ref=dst, send_sem=sems.at[0], recv_sem=sems.at[1], device_id=(sib, me), device_id_type=MESH
+        )
+
+    def y_copy(src, dst, sems):
+        return pltpu.make_async_remote_copy(
+            src_ref=src, dst_ref=dst, send_sem=sems.at[0], recv_sem=sems.at[1], device_id=(ynb, me), device_id_type=MESH
+        )
+
+    def part_copy(c):
+        return sibling_copy(part_send.at[c], part_recv.at[c], p_sem.at[c])
+
+    def q_copy(c):
+        return y_copy(q_send.at[c], q_recv.at[c], q_sem.at[c])
+
+    def s_copy(c):
+        return y_copy(s_send.at[c], s_recv.at[c], s_sem.at[c])
+
+    def out_rows(k):
+        return pl.ds(pl.multiple_of(k * rows, rows), rows)
+
+    def final_copy(c):
+        return sibling_copy(res.at[c], out_hbm.at[out_rows(core), span(c)], f_sem.at[c])
+
+    def out_copy(c):
+        return pltpu.make_async_copy(res.at[c], out_hbm.at[out_rows(core), span(c)], o_sem.at[c])
+
+    def dot(a, b):
+        return jnp.dot(a, b, preferred_element_type=jnp.float32)
+
+    def dot_nt(a, b):
+        return lax.dot_general(a, b, (((1,), (1,)), ((), ())), preferred_element_type=jnp.float32)
+
+    def compute(c):
+        for far in (1, 2, 3):
+            other = (z + far) % 4
+            arrived(c, other * 2 + 1 - x)
+
+        @pl.when(c % 2 == 0)
+        def _():
+            arrived(c, z * 2 + 1 - x)
+
+        own_load(c).wait()
+        block = gq[c].reshape(micro * mine * 8, cols)
+        part_send[c] = dot(emb_t[out_rows(1 - core), :], block)
+        part_copy(c).start()
+        part_own[c] = dot(emb_t[out_rows(core), :], block)
+        sums = dot(onehot[...], block)
+        high = sums.astype(jnp.bfloat16)
+        rest = sums - high.astype(jnp.float32)
+        mid = rest.astype(jnp.bfloat16)
+        low = (rest - mid.astype(jnp.float32)).astype(jnp.bfloat16)
+        w_part = w[:, span(c)]
+        bucket[...] += dot_nt(high, w_part) + dot_nt(mid, w_part) + dot_nt(low, w_part)
+
+    def core_sum(c):
+        part_copy(c).wait_recv()
+        total = part_own[c] + part_recv[c]
+        top = jnp.maximum(jnp.max(jnp.abs(total), axis=0, keepdims=True), 1e-30)
+        codes = jnp.round(total * (32767.0 / top))
+        q_send[c] = codes.astype(jnp.int32).astype(jnp.int16)
+        s_send[c] = jnp.broadcast_to(top * (1.0 / 32767.0), s_send.shape[1:])
+        q_copy(c).start()
+        s_copy(c).start()
+
+    def finish(c):
+        q_copy(c).wait_recv()
+        s_copy(c).wait_recv()
+        here = q_send[c].astype(jnp.int32).astype(jnp.float32) * s_send[c][0:1, :]
+        there = q_recv[c].astype(jnp.int32).astype(jnp.float32) * s_recv[c][0:1, :]
+        res[c] = jnp.where(y == 0, here, there) + jnp.where(y == 0, there, here)
+        final_copy(c).start()
+        out_copy(c).start()
+
+    def guarded(c, stage):
+        @pl.when((c >= 0) & (c < CHUNKS))
+        def _():
+            stage(c)
+
+    def forward_stage(far):
+        def stage(c):
+            each_forward(c, far, start, True)
+            if far == 1:
+                each_relay(c, start, True)
+
+        return stage
+
+    for c in range(2):
+        each_own(c, start)
+
+    loads[0].wait()
+    group = mine * 8
+    for m in range(micro):
+        emb_t[:, m * group : (m + 1) * group] = emb[m].T
+    loads[1].wait()
+    bucket[...] = dot(onehot[:, 0:group], resid[0]) + dot(onehot[:, group : 2 * group], resid[1])
+    loads[2].wait()
+
+    def slot(s, carry):
+        guarded(s, lambda c: each_own(c, start))
+        guarded(s - 2, forward_stage(1))
+        guarded(s - 3, forward_stage(2))
+        guarded(s - 4, forward_stage(3))
+        guarded(s - 5, compute)
+        guarded(s - 6, core_sum)
+        guarded(s - 8, finish)
+        return carry
+
+    lax.fori_loop(2, CHUNKS + 5, slot, 0)
+
+    half = b_send.shape[1]
+
+    def half_cols(k):
+        return pl.ds(pl.multiple_of(k * half, half), half)
+
+    b_copy = sibling_copy(b_send, b_recv, b_sem)
+    b_send[...] = bucket[:, half_cols(1 - core)]
+    b_copy.start()
+    core_sum(CHUNKS - 1)
+    b_copy.wait_recv()
+    y_send[...] = bucket[:, half_cols(core)] + b_recv[...]
+    rows_copy = y_copy(y_send, y_recv, y_sem)
+    rows_copy.start()
+    finish(CHUNKS - 3)
+    rows_copy.wait_recv()
+    a_send[...] = y_send[...] + y_recv[...]
+
+    def a_copy(step):
+        to = (me + step) % 8
+        return pltpu.make_async_remote_copy(
+            src_ref=a_send.at[pl.ds(pl.multiple_of(to * SLOT, SLOT), SLOT), :],
+            dst_ref=a_recv.at[me],
+            send_sem=a_send_sem.at[step],
+            recv_sem=a_recv_sem.at[me],
+            device_id=(dp, to),
+            device_id_type=MESH,
+        )
+
+    def a_arrived(step):
+        origin = (me + 8 - step) % 8
+        return pltpu.make_async_remote_copy(
+            src_ref=a_send.at[pl.ds(0, SLOT), :],
+            dst_ref=a_recv.at[origin],
+            send_sem=a_send_sem.at[step],
+            recv_sem=a_recv_sem.at[origin],
+            device_id=(dp, origin),
+            device_id_type=MESH,
+        )
+
+    for step in range(1, 8):
+        a_copy(step).start()
+    a_recv[me] = a_send[pl.ds(pl.multiple_of(me * SLOT, SLOT), SLOT), :]
+    finish(CHUNKS - 2)
+    for step in range(1, 8):
+        a_arrived(step).wait_recv()
+    h_copy = sibling_copy(a_recv, sib_recv, h_sem)
+    h_copy.start()
+    finish(CHUNKS - 1)
+    h_copy.wait_recv()
+    for t in range(8):
+        for k in range(2):
+            at = (t % 2) * 2 * half + k * half
+            grads_out[t // 2, :, at : at + half] = jnp.where(core == k, a_recv[t], sib_recv[t])
+
+    h_copy.wait_send()
+    b_copy.wait_send()
+    rows_copy.wait_send()
+    for step in range(1, 8):
+        a_copy(step).wait_send()
+
+    def sent(copy):
+        copy.wait_send()
+
+    def drain(c, carry):
+        each_own(c, sent)
+        for far in (1, 2, 3):
+            each_forward(c, far, sent, False)
+        each_relay(c, sent, False)
+        part_copy(c).wait_send()
+        q_copy(c).wait_send()
+        s_copy(c).wait_send()
+        final_copy(c).wait()
+        out_copy(c).wait()
+        return carry
+
+    lax.fori_loop(0, CHUNKS, drain, 0)
+
+
+def fused(
+    embedded,
+    resid_grad,
+    query_grad,
+    query_weight,
+    ngram_rows,
+    touched_rows,
+    row_values,
+    row_mean,
+    row_square,
+):
+    micro, group, width = embedded.shape
+    hidden = query_grad.shape[2]
+    tables = touched_rows.shape[0]
+    table_idx = lax.axis_index("table")
+    slice_idx = table_idx * width // SW
+    entries = touched_rows.shape[2]
+    ids = lax.dynamic_index_in_dim(ngram_rows, slice_idx, 2, False).reshape(1, micro * group)
+    listed = lax.dynamic_index_in_dim(touched_rows, slice_idx, 1, False)
+    listed = jnp.pad(listed, ((0, 0), (0, SLOT - entries)), constant_values=-1).reshape(tables * SLOT, 1)
+    onehot = (listed == ids).astype(jnp.bfloat16)
+
+    cols, half, rows = hidden // CHUNKS, width // 2, width // 2
+    slots = tables * SLOT
+    f32, bf16, i16 = jnp.float32, jnp.bfloat16, jnp.int16
+    dma = pltpu.SemaphoreType.DMA
+    vmem = pltpu.VMEM
+    anywhere = pl.BlockSpec(memory_space=pl.ANY)
+    in_vmem = pl.BlockSpec(memory_space=pltpu.VMEM)
+    weight_grad, grads = pl.pallas_call(
+        kernel,
+        out_shape=(
+            jax.ShapeDtypeStruct((width, hidden), f32),
+            jax.ShapeDtypeStruct((SLICES, SLOT, SW), f32),
+        ),
+        in_specs=[anywhere] * 4 + [in_vmem],
+        out_specs=(anywhere, in_vmem),
+        scratch_shapes=[
+            vmem((micro, group, width), bf16),
+            vmem((width, micro * group), bf16),
+            vmem((micro, group, width), bf16),
+            vmem((width, hidden), bf16),
+            vmem((CHUNKS, micro, group, cols), bf16),
+            vmem((CHUNKS, rows, cols), f32),
+            vmem((CHUNKS, rows, cols), f32),
+            vmem((CHUNKS, rows, cols), f32),
+            vmem((CHUNKS, rows, cols), i16),
+            vmem((CHUNKS, rows, cols), i16),
+            vmem((CHUNKS, 8, cols), f32),
+            vmem((CHUNKS, 8, cols), f32),
+            vmem((CHUNKS, rows, cols), f32),
+            vmem((slots, width), f32),
+            vmem((slots, half), f32),
+            vmem((slots, half), f32),
+            vmem((slots, half), f32),
+            vmem((slots, half), f32),
+            vmem((slots, half), f32),
+            vmem((tables, SLOT, half), f32),
+            vmem((tables, SLOT, half), f32),
+            dma((3 + CHUNKS,)),
+            dma((CHUNKS, tables, 3)),
+            dma((CHUNKS, tables)),
+            dma((CHUNKS, 2)),
+            dma((CHUNKS, 2)),
+            dma((CHUNKS, 2)),
+            dma((CHUNKS, 2)),
+            dma((CHUNKS,)),
+            dma((2,)),
+            dma((2,)),
+            dma((tables,)),
+            dma((tables,)),
+            dma((2,)),
+        ],
+        compiler_params=pltpu.CompilerParams(
+            collective_id=0, has_side_effects=True, vmem_limit_bytes=40 * 1024 * 1024
+        ),
+        cost_estimate=pl.CostEstimate(flops=3 * 10**9, bytes_accessed=2 * 10**7, transcendentals=0),
+    )(embedded, resid_grad, query_grad, query_weight, onehot)
+
+    mine = lax.dynamic_index_in_dim(touched_rows, table_idx, 0, False)
+    live = (mine >= 0)[..., None]
+    values_next, mean_next, square_next = adam_rows(
+        grads[:, :entries], row_values[0], row_mean[0], row_square[0], live
+    )
+    return (weight_grad, values_next[None], mean_next[None], square_next[None])
+
+
 def solution(mesh):
     placed = (
         P(None, "dp", "table"),
@@ -109,8 +550,9 @@
         P("table", None, None, None),
         P("table", None, None, None),
     )
+    fits = mesh.shape["dp"] == 4 and mesh.shape["table"] == 8
     return jax.shard_map(
-        local,
+        fused if fits else local,
         mesh=mesh,
         in_specs=placed,
         out_specs=(

time: 233 us -> 84.6 us (0.36)
  waiting for transfers between devices: 187 us -> 0 us
  Pallas kernels: 0 us -> 71.8 us
  matrix products: 14.3 us -> 0 us
  between operations: 13.9 us -> 0.72 us
  starting transfers between devices: 3.53 us -> 0 us
    all_gather x2 -> x0, waiting for transfers between devices: 97.2 us -> none  [local(): lax.all_gather(query_grad[micro:micro + 1], 'table', axis=1, tiled=True)]
    psum x1 -> x0, waiting for transfers between devices: 87.4 us -> none  [local(): weight_grad = lax.psum(wgrad, 'dp')]
    pallas_call x0 -> x1, Pallas kernels: none -> 71.8 us  [fused(): pl.pallas_call(kernel, out_shape=(jax.ShapeDtypeStruct((width, hidden), f...]
    dot_general x5 -> x0, matrix products: 14.3 us -> none  [the longest x2 6.86 us: make_step(): jnp.einsum('mrh,ph->mrp', piece, weight_part, preferred_element_type=jnp....]
    unnamed x18 -> x20, local copies, waits for them, and re-layouts: 4.74 us -> 9.52 us
    all_to_all x1 -> x0, starting transfers between devices: 3.41 us -> none  [local(): lax.all_to_all(buckets, 'table', split_axis=0, concat_axis=0, tiled=True)]
  transfers between devices with their start and end apart: 4 -> 0, of which waited for: 4 -> 0; matrix products, arithmetic and copies ran while one was open for 5% -> 0% of each run, Pallas kernels for 0% -> 0%
where the time goes in v1:
time: 84.6 us; the launch traced here: 84.2 us
  Pallas kernels  71.8 us (85%)
  local copies, waits for them, and re-layouts  10.4 us (12%)
  other arithmetic  1.27 us (2%)
    pallas_call x1, Pallas kernels, fused(): pl.pallas_call(kernel, out_shape=(jax.ShapeDtypeStruct((width, hidden), f...  71.8 us
    unnamed x20, local copies, waits for them, and re-layouts  9.52 us

profile of v1, /device:TPU:0, one launch (start us, length us, event | category | flops | bytes accessed | tf_op | source)
XLA Modules:
  0.0 84.2 jit_solution(1311805718700333424)
XLA Ops:
  0.6 0.0 copy-start
  0.7 0.7 fusion.5
  1.4 0.0 copy-done
  1.4 0.7 constant_dynamic-slice_fusion.1
  2.1 0.1 eq.17
  2.2 0.1 compare_convert_fusion.onehot
  2.3 0.0 copy-start.1
  2.3 1.6 %copy-done.1 = bf16[512,2048]{1,0:T(8,128)(2,1)S(1)} copy-done((bf16[512,2048]{1,0:T(8,128)(2,1)S(1)}, bf16[512,2048]{1,0:T(8,128)(2,1)}, u32[]{:S(2)}) %copy-start.1) | copy-done | bytes 2097176
  3.9 0.0 copy-start.2
  3.9 1.2 %copy-done.2 = bf16[2,512,512]{2,1,0:T(8,128)(2,1)S(1)} copy-done((bf16[2,512,512]{2,1,0:T(8,128)(2,1)S(1)}, bf16[2,512,512]{2,1,0:T(8,128)(2,1)}, u32[]{:S(2)}) %copy-start.2) | copy-done | bytes 1048600
  5.1 0.0 copy-start.3
  5.1 1.2 %copy-done.3 = bf16[2,512,512]{2,1,0:T(8,128)(2,1)S(1)} copy-done((bf16[2,512,512]{2,1,0:T(8,128)(2,1)S(1)}, bf16[2,512,512]{2,1,0:T(8,128)(2,1)}, u32[]{:S(2)}) %copy-start.3) | copy-done | bytes 1048600
  6.4 0.0 copy-start.4
  6.4 1.0 %copy-done.4 = bf16[2,64,2048]{2,1,0:T(8,128)(2,1)S(1)} copy-done((bf16[2,64,2048]{2,1,0:T(8,128)(2,1)S(1)}, bf16[2,64,2048]{2,1,0:T(8,128)(2,1)}, u32[]{:S(2)}) %copy-start.4) | copy-done | bytes 524312
  7.4 0.0 copy-start.5
  7.4 0.0 copy-start.6
  7.4 0.0 copy-start.7
  7.4 71.8 %shard_map.120 = (f32[512,2048]{1,0:T(8,128)S(1)}, f32[4,16,1024]{2,1,0:T(8,128)S(1)}) custom-call(bf16[2,512,512]{2,1,0:T(8,128)(2,1)S(1)} %copy-done.2, bf16[2,512,512]{2,1,0:T(8,128)(2,1)S(1)} %copy-done.3, bf16[2,64,2048]{2,1,0:T(8,128)(2,1)S(1)} %copy-done.4, bf16[512,2048]{1,0:T(8,128)(2,1)S(1)} %copy-done.1, ...), custom_call_target="tpu_custom_call" | custom-call | flops 3000000000 | bytes 20000000 | tf_op jit(solution)/shard_map/pallas_call | solution.py:483
  79.3 0.0 copy-done.5
  79.3 0.0 copy-done.6
  79.3 0.0 copy-done.7
  79.3 0.5 fusion.2
  79.8 0.8 copy.19
  80.6 0.8 copy.17
  81.4 0.8 copy.18
  82.2 2.0 %copy.43 = f32[512,2048]{1,0:T(8,128)} copy(f32[512,2048]{1,0:T(8,128)S(1)} %get-tuple-element.19) | data formatting | bytes 8388608
  (2 shorter events, 0.0 us)
Async XLA Ops:
  0.6 0.7 copy-start
  2.3 1.6 %copy-start.1 = (bf16[512,2048]{1,0:T(8,128)(2,1)S(1)}, bf16[512,2048]{1,0:T(8,128)(2,1)}, u32[]{:S(2)}) copy-start(bf16[512,2048]{1,0:T(8,128)(2,1)} %w_hbm.1) | copy-start | bytes 6291460
  3.9 1.2 %copy-start.2 = (bf16[2,512,512]{2,1,0:T(8,128)(2,1)S(1)}, bf16[2,512,512]{2,1,0:T(8,128)(2,1)}, u32[]{:S(2)}) copy-start(bf16[2,512,512]{2,1,0:T(8,128)(2,1)} %emb_hbm.1) | copy-start | bytes 3145732
  5.1 1.2 %copy-start.3 = (bf16[2,512,512]{2,1,0:T(8,128)(2,1)S(1)}, bf16[2,512,512]{2,1,0:T(8,128)(2,1)}, u32[]{:S(2)}) copy-start(bf16[2,512,512]{2,1,0:T(8,128)(2,1)} %resid_hbm.1) | copy-start | bytes 3145732
  6.4 1.0 %copy-start.4 = (bf16[2,64,2048]{2,1,0:T(8,128)(2,1)S(1)}, bf16[2,64,2048]{2,1,0:T(8,128)(2,1)}, u32[]{:S(2)}) copy-start(bf16[2,64,2048]{2,1,0:T(8,128)(2,1)} %qg_hbm.1) | copy-start | bytes 1572868
  7.4 71.9 %copy-start.5 = (f32[1,4,12,1024]{3,1,2,0:T(4,128)S(1)}, f32[1,4,12,1024]{3,1,2,0:T(4,128)}, u32[]{:S(2)}) copy-start(f32[1,4,12,1024]{3,1,2,0:T(4,128)} %param.17) | copy-start | bytes 589828
  7.4 71.9 %copy-start.6 = (f32[1,4,12,1024]{3,1,2,0:T(4,128)S(1)}, f32[1,4,12,1024]{3,1,2,0:T(4,128)}, u32[]{:S(2)}) copy-start(f32[1,4,12,1024]{3,1,2,0:T(4,128)} %param.16) | copy-start | bytes 589828
  7.4 71.9 %copy-start.7 = (f32[1,4,12,1024]{3,1,2,0:T(4,128)S(1)}, f32[1,4,12,1024]{3,1,2,0:T(4,128)}, u32[]{:S(2)}) copy-start(f32[1,4,12,1024]{3,1,2,0:T(4,128)} %param.15) | copy-start | bytes 589828

commit v2 on v1

--- a/solution.py
+++ b/solution.py
@@ -112,9 +112,15 @@
     resid_hbm,
     qg_hbm,
     w_hbm,
-    onehot,
+    ids_hbm,
+    touched_hbm,
     out_hbm,
     grads_out,
+    live_out,
+    ids,
+    touched,
+    lists,
+    onehot,
     emb,
     emb_t,
     resid,
@@ -170,9 +176,9 @@
         pltpu.make_async_copy(emb_hbm, emb, load_sem.at[0]),
         pltpu.make_async_copy(resid_hbm, resid, load_sem.at[1]),
         pltpu.make_async_copy(w_hbm, w, load_sem.at[2]),
+        pltpu.make_async_copy(ids_hbm, ids, load_sem.at[3]),
+        pltpu.make_async_copy(touched_hbm, touched, load_sem.at[4]),
     ]
-    for load in loads:
-        load.start()
 
     def span(c):
         return pl.ds(pl.multiple_of(c * cols, cols), cols)
@@ -184,10 +190,7 @@
         return gq.at[c, :, tokens(t), :]
 
     def own_load(c):
-        return pltpu.make_async_copy(qg_hbm.at[:, :, span(c)], held(c, me), load_sem.at[3 + c])
-
-    for c in range(CHUNKS):
-        own_load(c).start()
+        return pltpu.make_async_copy(qg_hbm.at[:, :, span(c)], held(c, me), load_sem.at[5 + c])
 
     pl.semaphore_wait(barrier, 9)
 
@@ -296,7 +299,7 @@
     def dot_nt(a, b):
         return lax.dot_general(a, b, (((1,), (1,)), ((), ())), preferred_element_type=jnp.float32)
 
-    def compute(c):
+    def compute(c, between=None):
         for far in (1, 2, 3):
             other = (z + far) % 4
             arrived(c, other * 2 + 1 - x)
@@ -307,9 +310,6 @@
 
         own_load(c).wait()
         block = gq[c].reshape(micro * mine * 8, cols)
-        part_send[c] = dot(emb_t[out_rows(1 - core), :], block)
-        part_copy(c).start()
-        part_own[c] = dot(emb_t[out_rows(core), :], block)
         sums = dot(onehot[...], block)
         high = sums.astype(jnp.bfloat16)
         rest = sums - high.astype(jnp.float32)
@@ -317,6 +317,11 @@
         low = (rest - mid.astype(jnp.float32)).astype(jnp.bfloat16)
         w_part = w[:, span(c)]
         bucket[...] += dot_nt(high, w_part) + dot_nt(mid, w_part) + dot_nt(low, w_part)
+        if between is not None:
+            between()
+        part_send[c] = dot(emb_t[out_rows(1 - core), :], block)
+        part_copy(c).start()
+        part_own[c] = dot(emb_t[out_rows(core), :], block)
 
     def core_sum(c):
         part_copy(c).wait_recv()
@@ -352,13 +357,36 @@
 
     for c in range(2):
         each_own(c, start)
-
+    for at in (4, 3, 1, 0, 2):
+        loads[at].start()
+    for c in range(CHUNKS):
+        own_load(c).start()
+
+    group = mine * 8
+    width = emb_t.shape[0]
+    entries = touched.shape[2]
+    slice_idx = me * width // SW
+    loads[4].wait()
+    lists[...] = jnp.full(lists.shape, -1.0, jnp.float32)
+    listed = touched[:, 0, :]
+    for s in range(1, SLICES):
+        listed = jnp.where(slice_idx == s, touched[:, s, :], listed)
+    lists[0:8, 0:entries] = listed.astype(jnp.float32)
+    lists[8 : 8 + SLICES, 0:entries] = touched[me].astype(jnp.float32)
+    columns = lists[...].T
+    for s in range(SLICES):
+        live_out[:, s, :] = jnp.broadcast_to(columns[0:entries, 8 + s : 9 + s], (entries, live_out.shape[2]))
+    loads[3].wait()
+    for m in range(micro):
+        row = ids[m, pl.ds(slice_idx, 1), :].astype(jnp.float32)
+        for o in range(8):
+            hit = columns[0:SLOT, o : o + 1] == row
+            onehot[o * SLOT : (o + 1) * SLOT, m * group : (m + 1) * group] = jnp.where(hit, 1.0, 0.0).astype(jnp.bfloat16)
+    loads[1].wait()
+    bucket[...] = dot(onehot[:, 0:group], resid[0]) + dot(onehot[:, group : 2 * group], resid[1])
     loads[0].wait()
-    group = mine * 8
     for m in range(micro):
         emb_t[:, m * group : (m + 1) * group] = emb[m].T
-    loads[1].wait()
-    bucket[...] = dot(onehot[:, 0:group], resid[0]) + dot(onehot[:, group : 2 * group], resid[1])
     loads[2].wait()
 
     def slot(s, carry):
@@ -371,7 +399,7 @@
         guarded(s - 8, finish)
         return carry
 
-    lax.fori_loop(2, CHUNKS + 5, slot, 0)
+    lax.fori_loop(2, CHUNKS + 4, slot, 0)
 
     half = b_send.shape[1]
 
@@ -379,13 +407,19 @@
         return pl.ds(pl.multiple_of(k * half, half), half)
 
     b_copy = sibling_copy(b_send, b_recv, b_sem)
-    b_send[...] = bucket[:, half_cols(1 - core)]
-    b_copy.start()
-    core_sum(CHUNKS - 1)
+
+    def send_bucket():
+        b_send[...] = bucket[:, half_cols(1 - core)]
+        b_copy.start()
+
+    compute(CHUNKS - 1, send_bucket)
+    core_sum(CHUNKS - 2)
     b_copy.wait_recv()
     y_send[...] = bucket[:, half_cols(core)] + b_recv[...]
     rows_copy = y_copy(y_send, y_recv, y_sem)
     rows_copy.start()
+    core_sum(CHUNKS - 1)
+    finish(CHUNKS - 4)
     finish(CHUNKS - 3)
     rows_copy.wait_recv()
     a_send[...] = y_send[...] + y_recv[...]
@@ -425,7 +459,8 @@
     for t in range(8):
         for k in range(2):
             at = (t % 2) * 2 * half + k * half
-            grads_out[t // 2, :, at : at + half] = jnp.where(core == k, a_recv[t], sib_recv[t])
+            piece = jnp.where(core == k, a_recv[t], sib_recv[t])
+            grads_out[:, t // 2, at : at + half] = piece[0:entries]
 
     h_copy.wait_send()
     b_copy.wait_send()
@@ -465,30 +500,31 @@
     micro, group, width = embedded.shape
     hidden = query_grad.shape[2]
     tables = touched_rows.shape[0]
-    table_idx = lax.axis_index("table")
-    slice_idx = table_idx * width // SW
     entries = touched_rows.shape[2]
-    ids = lax.dynamic_index_in_dim(ngram_rows, slice_idx, 2, False).reshape(1, micro * group)
-    listed = lax.dynamic_index_in_dim(touched_rows, slice_idx, 1, False)
-    listed = jnp.pad(listed, ((0, 0), (0, SLOT - entries)), constant_values=-1).reshape(tables * SLOT, 1)
-    onehot = (listed == ids).astype(jnp.bfloat16)
-
     cols, half, rows = hidden // CHUNKS, width // 2, width // 2
     slots = tables * SLOT
     f32, bf16, i16 = jnp.float32, jnp.bfloat16, jnp.int16
     dma = pltpu.SemaphoreType.DMA
     vmem = pltpu.VMEM
     anywhere = pl.BlockSpec(memory_space=pl.ANY)
+    in_hbm = pl.BlockSpec(memory_space=pltpu.HBM)
     in_vmem = pl.BlockSpec(memory_space=pltpu.VMEM)
-    weight_grad, grads = pl.pallas_call(
+    operands = (embedded, resid_grad, query_grad, query_weight, ngram_rows.transpose(0, 2, 1), touched_rows)
+    operands = [pltpu.with_memory_space_constraint(operand, pltpu.HBM) for operand in operands]
+    weight_grad, grads, lists = pl.pallas_call(
         kernel,
         out_shape=(
             jax.ShapeDtypeStruct((width, hidden), f32),
-            jax.ShapeDtypeStruct((SLICES, SLOT, SW), f32),
+            jax.ShapeDtypeStruct((entries, SLICES, SW), f32),
+            jax.ShapeDtypeStruct((entries, SLICES, SW), f32),
         ),
-        in_specs=[anywhere] * 4 + [in_vmem],
-        out_specs=(anywhere, in_vmem),
+        in_specs=[in_hbm] * 6,
+        out_specs=(anywhere, in_vmem, in_vmem),
         scratch_shapes=[
+            vmem((micro, SLICES, group), jnp.int32),
+            vmem(touched_rows.shape, jnp.int32),
+            vmem((128, 128), f32),
+            vmem((slots, micro * group), bf16),
             vmem((micro, group, width), bf16),
             vmem((width, micro * group), bf16),
             vmem((micro, group, width), bf16),
@@ -510,7 +546,7 @@
             vmem((slots, half), f32),
             vmem((tables, SLOT, half), f32),
             vmem((tables, SLOT, half), f32),
-            dma((3 + CHUNKS,)),
+            dma((5 + CHUNKS,)),
             dma((CHUNKS, tables, 3)),
             dma((CHUNKS, tables)),
             dma((CHUNKS, 2)),
@@ -528,14 +564,14 @@
             collective_id=0, has_side_effects=True, vmem_limit_bytes=40 * 1024 * 1024
         ),
         cost_estimate=pl.CostEstimate(flops=3 * 10**9, bytes_accessed=2 * 10**7, transcendentals=0),
-    )(embedded, resid_grad, query_grad, query_weight, onehot)
-
-    mine = lax.dynamic_index_in_dim(touched_rows, table_idx, 0, False)
-    live = (mine >= 0)[..., None]
-    values_next, mean_next, square_next = adam_rows(
-        grads[:, :entries], row_values[0], row_mean[0], row_square[0], live
-    )
-    return (weight_grad, values_next[None], mean_next[None], square_next[None])
+    )(*operands)
+
+    def turned(rows):
+        return rows[0].transpose(1, 0, 2)
+
+    after = adam_rows(grads, turned(row_values), turned(row_mean), turned(row_square), lists >= 0)
+    values_next, mean_next, square_next = [rows.transpose(1, 0, 2)[None] for rows in after]
+    return (weight_grad, values_next, mean_next, square_next)
 
 
 def solution(mesh):

time: 84.6 us -> 75.1 us (0.89)
  local copies, waits for them, and re-layouts: 10.4 us -> 2.03 us
  Pallas kernels: 71.8 us -> 70.3 us
    unnamed x20 -> x7, local copies, waits for them, and re-layouts: 9.52 us -> 2.03 us
    pallas_call x1, Pallas kernels: 71.8 us -> 70.3 us  [fused(): pl.pallas_call(kernel, out_shape=(jax.ShapeDtypeStruct((width, hidden), f...]
    broadcast_in_dim x1 -> x2, other arithmetic: 0.46 us -> 1.89 us  [fused(): rows.transpose(1, 0, 2)[None]]
where the time goes in v2:
time: 75.1 us; the launch traced here: 74.9 us
  Pallas kernels  70.3 us (94%)
  local copies, waits for them, and re-layouts  2.03 us (3%)
  other arithmetic  1.89 us (3%)
    pallas_call x1, Pallas kernels, fused(): pl.pallas_call(kernel, out_shape=(jax.ShapeDtypeStruct((width, hidden), f...  70.3 us
    unnamed x7, local copies, waits for them, and re-layouts  2.03 us
    broadcast_in_dim x2, other arithmetic, fused(): rows.transpose(1, 0, 2)[None]  1.89 us

profile of v2, /device:TPU:0, one launch (start us, length us, event | category | flops | bytes accessed | tf_op | source)
XLA Modules:
  0.0 74.9 jit_solution(8200754797782128839)
XLA Ops:
  0.6 0.0 copy-start
  0.6 0.0 copy-start.1
  0.7 0.0 copy-start.2
  0.7 70.3 %shard_map.120 = (f32[512,2048]{1,0:T(8,128)S(1)}, f32[12,4,1024]{2,1,0:T(4,128)S(1)}, f32[12,4,1024]{2,1,0:T(4,128)S(1)}) custom-call(bf16[2,512,512]{2,1,0:T(8,128)(2,1)} %emb_hbm.1, bf16[2,512,512]{2,1,0:T(8,128)(2,1)} %resid_hbm.1, bf16[2,64,2048]{2,1,0:T(8,128)(2,1)} %qg_hbm.1, bf16[512,2048]{1,0:T(8,128)(2,1)} %w_hbm.1, s32[2,4,512]{2,1,0:T(4,128)} %bitcast.43, ...), custom_call_target="tpu_custom_call" | custom-call | flops 3000000000 | bytes 20000000 | tf_op jit(solution)/shard_map/pallas_call | solution.py:514
  71.0 0.0 copy-done
  71.0 0.8 %fusion.2 = (f32[1,4,12,1024]{3,1,2,0:T(4,128)}, pred[12,4,1024]{2,1,0:T(4,128)(4,1)S(1)}) fusion(f32[1,4,12,1024]{3,1,2,0:T(4,128)S(1)} %copy-done, f32[12,4,1024]{2,1,0:T(4,128)S(1)} %get-tuple-element.9, f32[12,4,1024]{2,1,0:T(4,128)S(1)} %get-tuple-element.8), kind=kLoop, calls=%fused_computation.6 | loop fusion | flops 294912 | bytes 835584 | tf_op jit(solution)/shard_map/broadcast_in_dim | solution.py:573
  71.8 0.0 copy-done.1
  71.8 0.0 copy-done.2
  71.8 1.1 %fusion.4 = (f32[1,4,12,1024]{3,1,2,0:T(4,128)}, f32[1,4,12,1024]{3,1,2,0:T(4,128)}) fusion(pred[12,4,1024]{2,1,0:T(4,128)(4,1)S(1)} %get-tuple-element.11, f32[1,4,12,1024]{3,1,2,0:T(4,128)S(1)} %copy-done.1, f32[12,4,1024]{2,1,0:T(4,128)S(1)} %get-tuple-element.9, f32[1,4,12,1024]{3,1,2,0:T(4,128)S(1)} %copy-done, f32[1,4,12,1024]{3,1,2,0:T(4,128)S(1)} %copy-done.2), kind=kLoop, calls=%fused_computation.10 | loop fusion | flops 688128 | bytes 1228800 | tf_op jit(solution)/shard_map/broadcast_in_dim | solution.py:573
  72.9 2.0 %copy.14 = f32[512,2048]{1,0:T(8,128)} copy(f32[512,2048]{1,0:T(8,128)S(1)} %get-tuple-element.18) | data formatting | bytes 8388608
Async XLA Ops:
  0.6 70.4 %copy-start = (f32[1,4,12,1024]{3,1,2,0:T(4,128)S(1)}, f32[1,4,12,1024]{3,1,2,0:T(4,128)}, u32[]{:S(2)}) copy-start(f32[1,4,12,1024]{3,1,2,0:T(4,128)} %param.17) | copy-start | bytes 589828
  0.6 71.2 %copy-start.1 = (f32[1,4,12,1024]{3,1,2,0:T(4,128)S(1)}, f32[1,4,12,1024]{3,1,2,0:T(4,128)}, u32[]{:S(2)}) copy-start(f32[1,4,12,1024]{3,1,2,0:T(4,128)} %param.16) | copy-start | bytes 589828
  0.7 71.2 %copy-start.2 = (f32[1,4,12,1024]{3,1,2,0:T(4,128)S(1)}, f32[1,4,12,1024]{3,1,2,0:T(4,128)}, u32[]{:S(2)}) copy-start(f32[1,4,12,1024]{3,1,2,0:T(4,128)} %param.15) | copy-start | bytes 589828

commit v3 on v2

--- a/solution.py
+++ b/solution.py
@@ -392,14 +392,14 @@
     def slot(s, carry):
         guarded(s, lambda c: each_own(c, start))
         guarded(s - 2, forward_stage(1))
-        guarded(s - 3, forward_stage(2))
-        guarded(s - 4, forward_stage(3))
-        guarded(s - 5, compute)
-        guarded(s - 6, core_sum)
-        guarded(s - 8, finish)
+        guarded(s - 4, forward_stage(2))
+        guarded(s - 6, forward_stage(3))
+        guarded(s - 8, compute)
+        guarded(s - 9, core_sum)
+        guarded(s - 10, finish)
         return carry
 
-    lax.fori_loop(2, CHUNKS + 4, slot, 0)
+    lax.fori_loop(2, CHUNKS + 7, slot, 0)
 
     half = b_send.shape[1]
 
@@ -419,7 +419,6 @@
     rows_copy = y_copy(y_send, y_recv, y_sem)
     rows_copy.start()
     core_sum(CHUNKS - 1)
-    finish(CHUNKS - 4)
     finish(CHUNKS - 3)
     rows_copy.wait_recv()
     a_send[...] = y_send[...] + y_recv[...]

time: 75.1 us -> 81 us (1.079)
  Pallas kernels: 70.3 us -> 76.3 us
    pallas_call x1, Pallas kernels: 70.3 us -> 76.3 us  [fused(): pl.pallas_call(kernel, out_shape=(jax.ShapeDtypeStruct((width, hidden), f...]
where the time goes in v3:
time: 81 us; the launch traced here: 80.9 us
  Pallas kernels  76.3 us (94%)
  local copies, waits for them, and re-layouts  2.03 us (3%)
  other arithmetic  1.89 us (2%)
    pallas_call x1, Pallas kernels, fused(): pl.pallas_call(kernel, out_shape=(jax.ShapeDtypeStruct((width, hidden), f...  76.3 us
    unnamed x7, local copies, waits for them, and re-layouts  2.03 us
    broadcast_in_dim x2, other arithmetic, fused(): rows.transpose(1, 0, 2)[None]  1.89 us

profile of v3, /device:TPU:0, one launch (start us, length us, event | category | flops | bytes accessed | tf_op | source)
XLA Modules:
  0.0 80.9 jit_solution(11068024163067849161)
XLA Ops:
  0.6 0.0 copy-start
  0.6 0.0 copy-start.1
  0.7 0.0 copy-start.2
  0.7 76.3 %shard_map.120 = (f32[512,2048]{1,0:T(8,128)S(1)}, f32[12,4,1024]{2,1,0:T(4,128)S(1)}, f32[12,4,1024]{2,1,0:T(4,128)S(1)}) custom-call(bf16[2,512,512]{2,1,0:T(8,128)(2,1)} %emb_hbm.1, bf16[2,512,512]{2,1,0:T(8,128)(2,1)} %resid_hbm.1, bf16[2,64,2048]{2,1,0:T(8,128)(2,1)} %qg_hbm.1, bf16[512,2048]{1,0:T(8,128)(2,1)} %w_hbm.1, s32[2,4,512]{2,1,0:T(4,128)} %bitcast.43, ...), custom_call_target="tpu_custom_call" | custom-call | flops 3000000000 | bytes 20000000 | tf_op jit(solution)/shard_map/pallas_call | solution.py:513
  77.0 0.0 copy-done
  77.0 0.8 %fusion.2 = (f32[1,4,12,1024]{3,1,2,0:T(4,128)}, pred[12,4,1024]{2,1,0:T(4,128)(4,1)S(1)}) fusion(f32[1,4,12,1024]{3,1,2,0:T(4,128)S(1)} %copy-done, f32[12,4,1024]{2,1,0:T(4,128)S(1)} %get-tuple-element.9, f32[12,4,1024]{2,1,0:T(4,128)S(1)} %get-tuple-element.8), kind=kLoop, calls=%fused_computation.6 | loop fusion | flops 294912 | bytes 835584 | tf_op jit(solution)/shard_map/broadcast_in_dim | solution.py:572
  77.8 0.0 copy-done.1
  77.8 0.0 copy-done.2
  77.8 1.1 %fusion.4 = (f32[1,4,12,1024]{3,1,2,0:T(4,128)}, f32[1,4,12,1024]{3,1,2,0:T(4,128)}) fusion(pred[12,4,1024]{2,1,0:T(4,128)(4,1)S(1)} %get-tuple-element.11, f32[1,4,12,1024]{3,1,2,0:T(4,128)S(1)} %copy-done.1, f32[12,4,1024]{2,1,0:T(4,128)S(1)} %get-tuple-element.9, f32[1,4,12,1024]{3,1,2,0:T(4,128)S(1)} %copy-done, f32[1,4,12,1024]{3,1,2,0:T(4,128)S(1)} %copy-done.2), kind=kLoop, calls=%fused_computation.10 | loop fusion | flops 688128 | bytes 1228800 | tf_op jit(solution)/shard_map/broadcast_in_dim | solution.py:572
  78.9 2.0 %copy.14 = f32[512,2048]{1,0:T(8,128)} copy(f32[512,2048]{1,0:T(8,128)S(1)} %get-tuple-element.18) | data formatting | bytes 8388608
Async XLA Ops:
  0.6 76.3 %copy-start = (f32[1,4,12,1024]{3,1,2,0:T(4,128)S(1)}, f32[1,4,12,1024]{3,1,2,0:T(4,128)}, u32[]{:S(2)}) copy-start(f32[1,4,12,1024]{3,1,2,0:T(4,128)} %param.17) | copy-start | bytes 589828
  0.6 77.2 %copy-start.1 = (f32[1,4,12,1024]{3,1,2,0:T(4,128)S(1)}, f32[1,4,12,1024]{3,1,2,0:T(4,128)}, u32[]{:S(2)}) copy-start(f32[1,4,12,1024]{3,1,2,0:T(4,128)} %param.16) | copy-start | bytes 589828
  0.7 77.2 %copy-start.2 = (f32[1,4,12,1024]{3,1,2,0:T(4,128)S(1)}, f32[1,4,12,1024]{3,1,2,0:T(4,128)}, u32[]{:S(2)}) copy-start(f32[1,4,12,1024]{3,1,2,0:T(4,128)} %param.15) | copy-start | bytes 589828

commit v4 on v2

--- a/solution.py
+++ b/solution.py
@@ -101,6 +101,7 @@
     return (weight_grad, values_next[None], mean_next[None], square_next[None])
 
 
+LEAD = 4
 CHUNKS = 8
 SLOT = 16
 MESH = pl.DeviceIdType.MESH
@@ -316,7 +317,9 @@
         mid = rest.astype(jnp.bfloat16)
         low = (rest - mid.astype(jnp.float32)).astype(jnp.bfloat16)
         w_part = w[:, span(c)]
-        bucket[...] += dot_nt(high, w_part) + dot_nt(mid, w_part) + dot_nt(low, w_part)
+        terms = dot_nt(jnp.concatenate([high, mid, low], axis=0), w_part)
+        slots = bucket.shape[0]
+        bucket[...] += terms[0:slots] + terms[slots : 2 * slots] + terms[2 * slots : 3 * slots]
         if between is not None:
             between()
         part_send[c] = dot(emb_t[out_rows(1 - core), :], block)
@@ -355,7 +358,7 @@
 
         return stage
 
-    for c in range(2):
+    for c in range(LEAD):
         each_own(c, start)
     for at in (4, 3, 1, 0, 2):
         loads[at].start()
@@ -389,17 +392,39 @@
         emb_t[:, m * group : (m + 1) * group] = emb[m].T
     loads[2].wait()
 
+    def sent(copy):
+        copy.wait_send()
+
+    def drain(c):
+        each_own(c, sent)
+        for far in (1, 2, 3):
+            each_forward(c, far, sent, False)
+        each_relay(c, sent, False)
+        part_copy(c).wait_send()
+        q_copy(c).wait_send()
+        s_copy(c).wait_send()
+        final_copy(c).wait()
+        out_copy(c).wait()
+
     def slot(s, carry):
-        guarded(s, lambda c: each_own(c, start))
-        guarded(s - 2, forward_stage(1))
-        guarded(s - 3, forward_stage(2))
-        guarded(s - 4, forward_stage(3))
-        guarded(s - 5, compute)
-        guarded(s - 6, core_sum)
-        guarded(s - 8, finish)
+        guarded(s + LEAD - 1, lambda c: each_own(c, start))
+        guarded(s - 1, forward_stage(1))
+        guarded(s - 2, forward_stage(2))
+        guarded(s - 3, forward_stage(3))
+        guarded(s - 4, compute)
+        guarded(s - 5, core_sum)
+        guarded(s - 7, finish)
+        guarded(s - 8, drain)
         return carry
 
-    lax.fori_loop(2, CHUNKS + 4, slot, 0)
+    lax.fori_loop(1, CHUNKS + 3, slot, 0)
+
+    def drain_some(low, high):
+        def one(c, carry):
+            drain(c)
+            return carry
+
+        lax.fori_loop(low, high, one, 0)
 
     half = b_send.shape[1]
 
@@ -420,6 +445,7 @@
     rows_copy.start()
     core_sum(CHUNKS - 1)
     finish(CHUNKS - 4)
+    drain_some(CHUNKS - 5, CHUNKS - 4)
     finish(CHUNKS - 3)
     rows_copy.wait_recv()
     a_send[...] = y_send[...] + y_recv[...]
@@ -450,11 +476,13 @@
         a_copy(step).start()
     a_recv[me] = a_send[pl.ds(pl.multiple_of(me * SLOT, SLOT), SLOT), :]
     finish(CHUNKS - 2)
+    drain_some(CHUNKS - 4, CHUNKS - 3)
     for step in range(1, 8):
         a_arrived(step).wait_recv()
     h_copy = sibling_copy(a_recv, sib_recv, h_sem)
     h_copy.start()
     finish(CHUNKS - 1)
+    drain_some(CHUNKS - 3, CHUNKS - 1)
     h_copy.wait_recv()
     for t in range(8):
         for k in range(2):
@@ -468,22 +496,7 @@
     for step in range(1, 8):
         a_copy(step).wait_send()
 
-    def sent(copy):
-        copy.wait_send()
-
-    def drain(c, carry):
-        each_own(c, sent)
-        for far in (1, 2, 3):
-            each_forward(c, far, sent, False)
-        each_relay(c, sent, False)
-        part_copy(c).wait_send()
-        q_copy(c).wait_send()
-        s_copy(c).wait_send()
-        final_copy(c).wait()
-        out_copy(c).wait()
-        return carry
-
-    lax.fori_loop(0, CHUNKS, drain, 0)
+    drain_some(CHUNKS - 1, CHUNKS)
 
 
 def fused(

time: 75.1 us -> 74.7 us (level)
  no operation moved by 1% of the time
where the time goes in v4:
time: 74.7 us; the launch traced here: 74.5 us
  Pallas kernels  69.9 us (94%)
  local copies, waits for them, and re-layouts  2.03 us (3%)
  other arithmetic  1.89 us (3%)
    pallas_call x1, Pallas kernels, fused(): pl.pallas_call(kernel, out_shape=(jax.ShapeDtypeStruct((width, hidden), f...  69.9 us
    unnamed x7, local copies, waits for them, and re-layouts  2.03 us
    broadcast_in_dim x2, other arithmetic, fused(): rows.transpose(1, 0, 2)[None]  1.89 us

profile of v4, /device:TPU:0, one launch (start us, length us, event | category | flops | bytes accessed | tf_op | source)
XLA Modules:
  0.0 74.5 jit_solution(10352718067022428101)
XLA Ops:
  0.6 0.0 copy-start
  0.6 0.0 copy-start.1
  0.7 0.0 copy-start.2
  0.7 69.9 %shard_map.120 = (f32[512,2048]{1,0:T(8,128)S(1)}, f32[12,4,1024]{2,1,0:T(4,128)S(1)}, f32[12,4,1024]{2,1,0:T(4,128)S(1)}) custom-call(bf16[2,512,512]{2,1,0:T(8,128)(2,1)} %emb_hbm.1, bf16[2,512,512]{2,1,0:T(8,128)(2,1)} %resid_hbm.1, bf16[2,64,2048]{2,1,0:T(8,128)(2,1)} %qg_hbm.1, bf16[512,2048]{1,0:T(8,128)(2,1)} %w_hbm.1, s32[2,4,512]{2,1,0:T(4,128)} %bitcast.43, ...), custom_call_target="tpu_custom_call" | custom-call | flops 3000000000 | bytes 20000000 | tf_op jit(solution)/shard_map/pallas_call | solution.py:527
  70.6 0.0 copy-done
  70.6 0.8 %fusion.2 = (f32[1,4,12,1024]{3,1,2,0:T(4,128)}, pred[12,4,1024]{2,1,0:T(4,128)(4,1)S(1)}) fusion(f32[1,4,12,1024]{3,1,2,0:T(4,128)S(1)} %copy-done, f32[12,4,1024]{2,1,0:T(4,128)S(1)} %get-tuple-element.9, f32[12,4,1024]{2,1,0:T(4,128)S(1)} %get-tuple-element.8), kind=kLoop, calls=%fused_computation.6 | loop fusion | flops 294912 | bytes 835584 | tf_op jit(solution)/shard_map/broadcast_in_dim | solution.py:586
  71.4 0.0 copy-done.1
  71.4 0.0 copy-done.2
  71.4 1.1 %fusion.4 = (f32[1,4,12,1024]{3,1,2,0:T(4,128)}, f32[1,4,12,1024]{3,1,2,0:T(4,128)}) fusion(pred[12,4,1024]{2,1,0:T(4,128)(4,1)S(1)} %get-tuple-element.11, f32[1,4,12,1024]{3,1,2,0:T(4,128)S(1)} %copy-done.1, f32[12,4,1024]{2,1,0:T(4,128)S(1)} %get-tuple-element.9, f32[1,4,12,1024]{3,1,2,0:T(4,128)S(1)} %copy-done, f32[1,4,12,1024]{3,1,2,0:T(4,128)S(1)} %copy-done.2), kind=kLoop, calls=%fused_computation.10 | loop fusion | flops 688128 | bytes 1228800 | tf_op jit(solution)/shard_map/broadcast_in_dim | solution.py:586
  72.5 2.0 %copy.14 = f32[512,2048]{1,0:T(8,128)} copy(f32[512,2048]{1,0:T(8,128)S(1)} %get-tuple-element.18) | data formatting | bytes 8388608
Async XLA Ops:
  0.6 70.0 %copy-start = (f32[1,4,12,1024]{3,1,2,0:T(4,128)S(1)}, f32[1,4,12,1024]{3,1,2,0:T(4,128)}, u32[]{:S(2)}) copy-start(f32[1,4,12,1024]{3,1,2,0:T(4,128)} %param.17) | copy-start | bytes 589828
  0.6 70.8 %copy-start.1 = (f32[1,4,12,1024]{3,1,2,0:T(4,128)S(1)}, f32[1,4,12,1024]{3,1,2,0:T(4,128)}, u32[]{:S(2)}) copy-start(f32[1,4,12,1024]{3,1,2,0:T(4,128)} %param.16) | copy-start | bytes 589828
  0.7 70.8 %copy-start.2 = (f32[1,4,12,1024]{3,1,2,0:T(4,128)S(1)}, f32[1,4,12,1024]{3,1,2,0:T(4,128)}, u32[]{:S(2)}) copy-start(f32[1,4,12,1024]{3,1,2,0:T(4,128)} %param.15) | copy-start | bytes 589828

commit v5 on v4

--- a/solution.py
+++ b/solution.py
@@ -101,8 +101,8 @@
     return (weight_grad, values_next[None], mean_next[None], square_next[None])
 
 
-LEAD = 4
-CHUNKS = 8
+LEAD = 6
+CHUNKS = 16
 SLOT = 16
 MESH = pl.DeviceIdType.MESH
 UP, DOWN, ACROSS = 0, 1, 2

time: 74.7 us -> 83.8 us (1.12)
  Pallas kernels: 69.9 us -> 79 us
    pallas_call x1, Pallas kernels: 69.9 us -> 79 us  [fused(): pl.pallas_call(kernel, out_shape=(jax.ShapeDtypeStruct((width, hidden), f...]
where the time goes in v5:
time: 83.8 us; the launch traced here: 83.6 us
  Pallas kernels  79 us (94%)
  local copies, waits for them, and re-layouts  2.03 us (2%)
  other arithmetic  1.89 us (2%)
    pallas_call x1, Pallas kernels, fused(): pl.pallas_call(kernel, out_shape=(jax.ShapeDtypeStruct((width, hidden), f...  79 us
    unnamed x7, local copies, waits for them, and re-layouts  2.03 us
    broadcast_in_dim x2, other arithmetic, fused(): rows.transpose(1, 0, 2)[None]  1.89 us

profile of v5, /device:TPU:0, one launch (start us, length us, event | category | flops | bytes accessed | tf_op | source)
XLA Modules:
  0.0 83.6 jit_solution(15991362911906892417)
XLA Ops:
  0.6 0.0 copy-start
  0.6 0.0 copy-start.1
  0.7 0.0 copy-start.2
  0.7 79.0 %shard_map.120 = (f32[512,2048]{1,0:T(8,128)S(1)}, f32[12,4,1024]{2,1,0:T(4,128)S(1)}, f32[12,4,1024]{2,1,0:T(4,128)S(1)}) custom-call(bf16[2,512,512]{2,1,0:T(8,128)(2,1)} %emb_hbm.1, bf16[2,512,512]{2,1,0:T(8,128)(2,1)} %resid_hbm.1, bf16[2,64,2048]{2,1,0:T(8,128)(2,1)} %qg_hbm.1, bf16[512,2048]{1,0:T(8,128)(2,1)} %w_hbm.1, s32[2,4,512]{2,1,0:T(4,128)} %bitcast.43, ...), custom_call_target="tpu_custom_call" | custom-call | flops 3000000000 | bytes 20000000 | tf_op jit(solution)/shard_map/pallas_call | solution.py:527
  79.7 0.0 copy-done
  79.7 0.8 fusion.2
  80.6 0.0 copy-done.1
  80.6 0.0 copy-done.2
  80.6 1.1 %fusion.4 = (f32[1,4,12,1024]{3,1,2,0:T(4,128)}, f32[1,4,12,1024]{3,1,2,0:T(4,128)}) fusion(pred[12,4,1024]{2,1,0:T(4,128)(4,1)S(1)} %get-tuple-element.11, f32[1,4,12,1024]{3,1,2,0:T(4,128)S(1)} %copy-done.1, f32[12,4,1024]{2,1,0:T(4,128)S(1)} %get-tuple-element.9, f32[1,4,12,1024]{3,1,2,0:T(4,128)S(1)} %copy-done, f32[1,4,12,1024]{3,1,2,0:T(4,128)S(1)} %copy-done.2), kind=kLoop, calls=%fused_computation.10 | loop fusion | flops 688128 | bytes 1228800 | tf_op jit(solution)/shard_map/broadcast_in_dim | solution.py:586
  81.6 2.0 %copy.14 = f32[512,2048]{1,0:T(8,128)} copy(f32[512,2048]{1,0:T(8,128)S(1)} %get-tuple-element.18) | data formatting | bytes 8388608
Async XLA Ops:
  0.6 79.1 %copy-start = (f32[1,4,12,1024]{3,1,2,0:T(4,128)S(1)}, f32[1,4,12,1024]{3,1,2,0:T(4,128)}, u32[]{:S(2)}) copy-start(f32[1,4,12,1024]{3,1,2,0:T(4,128)} %param.17) | copy-start | bytes 589828
  0.6 79.9 %copy-start.1 = (f32[1,4,12,1024]{3,1,2,0:T(4,128)S(1)}, f32[1,4,12,1024]{3,1,2,0:T(4,128)}, u32[]{:S(2)}) copy-start(f32[1,4,12,1024]{3,1,2,0:T(4,128)} %param.16) | copy-start | bytes 589828
  0.7 79.9 %copy-start.2 = (f32[1,4,12,1024]{3,1,2,0:T(4,128)S(1)}, f32[1,4,12,1024]{3,1,2,0:T(4,128)}, u32[]{:S(2)}) copy-start(f32[1,4,12,1024]{3,1,2,0:T(4,128)} %param.15) | copy-start | bytes 589828

commit v6 on v4

--- a/solution.py
+++ b/solution.py
@@ -101,7 +101,7 @@
     return (weight_grad, values_next[None], mean_next[None], square_next[None])
 
 
-LEAD = 4
+LEAD = 3
 CHUNKS = 8
 SLOT = 16
 MESH = pl.DeviceIdType.MESH
@@ -121,14 +121,12 @@
     ids,
     touched,
     lists,
-    onehot,
     emb,
-    emb_t,
+    left,
     resid,
     w,
     gq,
-    part_own,
-    part_send,
+    prod,
     part_recv,
     q_send,
     q_recv,
@@ -165,7 +163,8 @@
     zpair = z + 1 - 2 * (z % 2)
     micro, mine, hidden = qg_hbm.shape
     cols = hidden // CHUNKS
-    rows = emb_t.shape[0] // 2
+    width = emb.shape[2]
+    rows = width // 2
 
     barrier = pltpu.get_barrier_semaphore()
     for step in range(1, 8):
@@ -277,7 +276,7 @@
         )
 
     def part_copy(c):
-        return sibling_copy(part_send.at[c], part_recv.at[c], p_sem.at[c])
+        return sibling_copy(prod.at[c, 0:rows], part_recv.at[c], p_sem.at[c])
 
     def q_copy(c):
         return y_copy(q_send.at[c], q_recv.at[c], q_sem.at[c])
@@ -300,7 +299,7 @@
     def dot_nt(a, b):
         return lax.dot_general(a, b, (((1,), (1,)), ((), ())), preferred_element_type=jnp.float32)
 
-    def compute(c, between=None):
+    def compute(c):
         for far in (1, 2, 3):
             other = (z + far) % 4
             arrived(c, other * 2 + 1 - x)
@@ -311,24 +310,18 @@
 
         own_load(c).wait()
         block = gq[c].reshape(micro * mine * 8, cols)
-        sums = dot(onehot[...], block)
+        prod[c] = dot(left[...], block)
+        part_copy(c).start()
+        sums = prod[c, width:, :]
         high = sums.astype(jnp.bfloat16)
-        rest = sums - high.astype(jnp.float32)
-        mid = rest.astype(jnp.bfloat16)
-        low = (rest - mid.astype(jnp.float32)).astype(jnp.bfloat16)
-        w_part = w[:, span(c)]
-        terms = dot_nt(jnp.concatenate([high, mid, low], axis=0), w_part)
+        low = (sums - high.astype(jnp.float32)).astype(jnp.bfloat16)
+        terms = dot_nt(jnp.concatenate([high, low], axis=0), w[:, span(c)])
         slots = bucket.shape[0]
-        bucket[...] += terms[0:slots] + terms[slots : 2 * slots] + terms[2 * slots : 3 * slots]
-        if between is not None:
-            between()
-        part_send[c] = dot(emb_t[out_rows(1 - core), :], block)
-        part_copy(c).start()
-        part_own[c] = dot(emb_t[out_rows(core), :], block)
+        bucket[...] += terms[0:slots] + terms[slots : 2 * slots]
 
     def core_sum(c):
         part_copy(c).wait_recv()
-        total = part_own[c] + part_recv[c]
+        total = prod[c, rows:width, :] + part_recv[c]
         top = jnp.maximum(jnp.max(jnp.abs(total), axis=0, keepdims=True), 1e-30)
         codes = jnp.round(total * (32767.0 / top))
         q_send[c] = codes.astype(jnp.int32).astype(jnp.int16)
@@ -366,7 +359,6 @@
         own_load(c).start()
 
     group = mine * 8
-    width = emb_t.shape[0]
     entries = touched.shape[2]
     slice_idx = me * width // SW
     loads[4].wait()
@@ -384,12 +376,15 @@
         row = ids[m, pl.ds(slice_idx, 1), :].astype(jnp.float32)
         for o in range(8):
             hit = columns[0:SLOT, o : o + 1] == row
-            onehot[o * SLOT : (o + 1) * SLOT, m * group : (m + 1) * group] = jnp.where(hit, 1.0, 0.0).astype(jnp.bfloat16)
+            left[width + o * SLOT : width + (o + 1) * SLOT, m * group : (m + 1) * group] = jnp.where(hit, 1.0, 0.0).astype(jnp.bfloat16)
     loads[1].wait()
-    bucket[...] = dot(onehot[:, 0:group], resid[0]) + dot(onehot[:, group : 2 * group], resid[1])
+    bucket[...] = dot(left[width:, 0:group], resid[0]) + dot(left[width:, group : 2 * group], resid[1])
     loads[0].wait()
     for m in range(micro):
-        emb_t[:, m * group : (m + 1) * group] = emb[m].T
+        for k in range(2):
+            first = rows * (1 - core) if k == 0 else rows * core
+            block = emb[m, :, k * rows : (k + 1) * rows].T
+            left[pl.ds(pl.multiple_of(first, rows), rows), m * group : (m + 1) * group] = block
     loads[2].wait()
 
     def sent(copy):
@@ -432,12 +427,9 @@
         return pl.ds(pl.multiple_of(k * half, half), half)
 
     b_copy = sibling_copy(b_send, b_recv, b_sem)
-
-    def send_bucket():
-        b_send[...] = bucket[:, half_cols(1 - core)]
-        b_copy.start()
-
-    compute(CHUNKS - 1, send_bucket)
+    compute(CHUNKS - 1)
+    b_send[...] = bucket[:, half_cols(1 - core)]
+    b_copy.start()
     core_sum(CHUNKS - 2)
     b_copy.wait_recv()
     y_send[...] = bucket[:, half_cols(core)] + b_recv[...]
@@ -537,14 +529,12 @@
             vmem((micro, SLICES, group), jnp.int32),
             vmem(touched_rows.shape, jnp.int32),
             vmem((128, 128), f32),
-            vmem((slots, micro * group), bf16),
             vmem((micro, group, width), bf16),
-            vmem((width, micro * group), bf16),
+            vmem((width + slots, micro * group), bf16),
             vmem((micro, group, width), bf16),
             vmem((width, hidden), bf16),
             vmem((CHUNKS, micro, group, cols), bf16),
-            vmem((CHUNKS, rows, cols), f32),
-            vmem((CHUNKS, rows, cols), f32),
+            vmem((CHUNKS, width + slots, cols), f32),
             vmem((CHUNKS, rows, cols), f32),
             vmem((CHUNKS, rows, cols), i16),
             vmem((CHUNKS, rows, cols), i16),

time: 74.7 us -> 74.5 us (level)
  no operation moved by 1% of the time
where the time goes in v6:
time: 74.5 us; the launch traced here: 74.4 us
  Pallas kernels  69.8 us (94%)
  local copies, waits for them, and re-layouts  2.03 us (3%)
  other arithmetic  1.89 us (3%)
    pallas_call x1, Pallas kernels, fused(): pl.pallas_call(kernel, out_shape=(jax.ShapeDtypeStruct((width, hidden), f...  69.8 us
    unnamed x7, local copies, waits for them, and re-layouts  2.03 us
    broadcast_in_dim x2, other arithmetic, fused(): rows.transpose(1, 0, 2)[None]  1.89 us

profile of v6, /device:TPU:0, one launch (start us, length us, event | category | flops | bytes accessed | tf_op | source)
XLA Modules:
  0.0 74.4 jit_solution(5422300266173952931)
XLA Ops:
  0.6 0.0 copy-start
  0.6 0.0 copy-start.1
  0.7 0.0 copy-start.2
  0.7 69.8 %shard_map.120 = (f32[512,2048]{1,0:T(8,128)S(1)}, f32[12,4,1024]{2,1,0:T(4,128)S(1)}, f32[12,4,1024]{2,1,0:T(4,128)S(1)}) custom-call(bf16[2,512,512]{2,1,0:T(8,128)(2,1)} %emb_hbm.1, bf16[2,512,512]{2,1,0:T(8,128)(2,1)} %resid_hbm.1, bf16[2,64,2048]{2,1,0:T(8,128)(2,1)} %qg_hbm.1, bf16[512,2048]{1,0:T(8,128)(2,1)} %w_hbm.1, s32[2,4,512]{2,1,0:T(4,128)} %bitcast.43, ...), custom_call_target="tpu_custom_call" | custom-call | flops 3000000000 | bytes 20000000 | tf_op jit(solution)/shard_map/pallas_call | solution.py:519
  70.5 0.0 copy-done
  70.5 0.8 %fusion.2 = (f32[1,4,12,1024]{3,1,2,0:T(4,128)}, pred[12,4,1024]{2,1,0:T(4,128)(4,1)S(1)}) fusion(f32[1,4,12,1024]{3,1,2,0:T(4,128)S(1)} %copy-done, f32[12,4,1024]{2,1,0:T(4,128)S(1)} %get-tuple-element.9, f32[12,4,1024]{2,1,0:T(4,128)S(1)} %get-tuple-element.8), kind=kLoop, calls=%fused_computation.6 | loop fusion | flops 294912 | bytes 835584 | tf_op jit(solution)/shard_map/broadcast_in_dim | solution.py:576
  71.3 0.0 copy-done.1
  71.3 0.0 copy-done.2
  71.3 1.1 %fusion.4 = (f32[1,4,12,1024]{3,1,2,0:T(4,128)}, f32[1,4,12,1024]{3,1,2,0:T(4,128)}) fusion(pred[12,4,1024]{2,1,0:T(4,128)(4,1)S(1)} %get-tuple-element.11, f32[1,4,12,1024]{3,1,2,0:T(4,128)S(1)} %copy-done.1, f32[12,4,1024]{2,1,0:T(4,128)S(1)} %get-tuple-element.9, f32[1,4,12,1024]{3,1,2,0:T(4,128)S(1)} %copy-done, f32[1,4,12,1024]{3,1,2,0:T(4,128)S(1)} %copy-done.2), kind=kLoop, calls=%fused_computation.10 | loop fusion | flops 688128 | bytes 1228800 | tf_op jit(solution)/shard_map/broadcast_in_dim | solution.py:576
  72.4 2.0 %copy.14 = f32[512,2048]{1,0:T(8,128)} copy(f32[512,2048]{1,0:T(8,128)S(1)} %get-tuple-element.18) | data formatting | bytes 8388608
Async XLA Ops:
  0.6 69.8 %copy-start = (f32[1,4,12,1024]{3,1,2,0:T(4,128)S(1)}, f32[1,4,12,1024]{3,1,2,0:T(4,128)}, u32[]{:S(2)}) copy-start(f32[1,4,12,1024]{3,1,2,0:T(4,128)} %param.17) | copy-start | bytes 589828
  0.6 70.7 %copy-start.1 = (f32[1,4,12,1024]{3,1,2,0:T(4,128)S(1)}, f32[1,4,12,1024]{3,1,2,0:T(4,128)}, u32[]{:S(2)}) copy-start(f32[1,4,12,1024]{3,1,2,0:T(4,128)} %param.16) | copy-start | bytes 589828
  0.7 70.7 %copy-start.2 = (f32[1,4,12,1024]{3,1,2,0:T(4,128)S(1)}, f32[1,4,12,1024]{3,1,2,0:T(4,128)}, u32[]{:S(2)}) copy-start(f32[1,4,12,1024]{3,1,2,0:T(4,128)} %param.15) | copy-start | bytes 589828

commit v7 on v6

--- a/solution.py
+++ b/solution.py
@@ -105,7 +105,8 @@
 CHUNKS = 8
 SLOT = 16
 MESH = pl.DeviceIdType.MESH
-UP, DOWN, ACROSS = 0, 1, 2
+UP, DOWN, ACROSS, UP_TWO, DOWN_TWO = range(5)
+HOPS = (1, -1, 0, 2, -2)
 
 
 def kernel(
@@ -192,13 +193,14 @@
     def own_load(c):
         return pltpu.make_async_copy(qg_hbm.at[:, :, span(c)], held(c, me), load_sem.at[5 + c])
 
+    for c in range(CHUNKS):
+        own_load(c).start()
     pl.semaphore_wait(barrier, 9)
 
-    def shard_copy(c, t, way, source=None):
-        to_z = z + 1 if way == UP else z - 1
-        to = (dp, to_z * 2 + x) if way != ACROSS else (dp, z * 2 + 1 - x)
+    def shard_copy(c, t, way):
+        to = (dp, (z + HOPS[way]) * 2 + x) if way != ACROSS else (dp, z * 2 + 1 - x)
         return pltpu.make_async_remote_copy(
-            src_ref=held(c, t) if source is None else source,
+            src_ref=held(c, t),
             dst_ref=held(c, t),
             send_sem=g_send_sem.at[c, t, way],
             recv_sem=g_recv_sem.at[c, t],
@@ -210,17 +212,16 @@
         shard_copy(c, t, ACROSS).wait_recv()
 
     def each_own(c, act):
-        own = qg_hbm.at[:, :, span(c)]
-
-        @pl.when(z < 3)
-        def _():
-            act(shard_copy(c, me, UP, own))
-
-        @pl.when(z > 0)
-        def _():
-            act(shard_copy(c, me, DOWN, own))
-
-        act(shard_copy(c, me, ACROSS, own))
+        act(shard_copy(c, me, ACROSS))
+        for way, there in ((UP, z < 3), (DOWN, z > 0), (UP_TWO, z < 2), (DOWN_TWO, z > 1)):
+
+            @pl.when(there)
+            def _():
+                act(shard_copy(c, me, way))
+
+    def send_own(c):
+        own_load(c).wait()
+        each_own(c, start)
 
     def each_forward(c, far, act, wait):
         for sign, way in ((-1, UP), (1, DOWN)):
@@ -234,9 +235,11 @@
                 if wait:
                     arrived(c, t)
 
-                @pl.when(onward)
-                def _():
-                    act(shard_copy(c, t, way))
+                if far == 2:
+
+                    @pl.when(onward)
+                    def _():
+                        act(shard_copy(c, t, way))
 
                 if far == 1:
 
@@ -308,7 +311,6 @@
         def _():
             arrived(c, z * 2 + 1 - x)
 
-        own_load(c).wait()
         block = gq[c].reshape(micro * mine * 8, cols)
         prod[c] = dot(left[...], block)
         part_copy(c).start()
@@ -352,11 +354,9 @@
         return stage
 
     for c in range(LEAD):
-        each_own(c, start)
+        send_own(c)
     for at in (4, 3, 1, 0, 2):
         loads[at].start()
-    for c in range(CHUNKS):
-        own_load(c).start()
 
     group = mine * 8
     entries = touched.shape[2]
@@ -402,17 +402,17 @@
         out_copy(c).wait()
 
     def slot(s, carry):
-        guarded(s + LEAD - 1, lambda c: each_own(c, start))
+        guarded(s + LEAD - 1, send_own)
         guarded(s - 1, forward_stage(1))
-        guarded(s - 2, forward_stage(2))
-        guarded(s - 3, forward_stage(3))
-        guarded(s - 4, compute)
-        guarded(s - 5, core_sum)
-        guarded(s - 7, finish)
-        guarded(s - 8, drain)
+        guarded(s - 1, forward_stage(2))
+        guarded(s - 2, forward_stage(3))
+        guarded(s - 3, compute)
+        guarded(s - 4, core_sum)
+        guarded(s - 6, finish)
+        guarded(s - 7, drain)
         return carry
 
-    lax.fori_loop(1, CHUNKS + 3, slot, 0)
+    lax.fori_loop(1, CHUNKS + 2, slot, 0)
 
     def drain_some(low, high):
         def one(c, carry):
@@ -550,7 +550,7 @@
             vmem((tables, SLOT, half), f32),
             vmem((tables, SLOT, half), f32),
             dma((5 + CHUNKS,)),
-            dma((CHUNKS, tables, 3)),
+            dma((CHUNKS, tables, 5)),
             dma((CHUNKS, tables)),
             dma((CHUNKS, 2)),
             dma((CHUNKS, 2)),

time: 74.5 us -> 76.2 us (1.023)
  Pallas kernels: 69.8 us -> 71.5 us
    pallas_call x1, Pallas kernels: 69.8 us -> 71.5 us  [fused(): pl.pallas_call(kernel, out_shape=(jax.ShapeDtypeStruct((width, hidden), f...]
where the time goes in v7:
time: 76.2 us; the launch traced here: 76.1 us
  Pallas kernels  71.5 us (94%)
  local copies, waits for them, and re-layouts  2.03 us (3%)
  other arithmetic  1.89 us (2%)
    pallas_call x1, Pallas kernels, fused(): pl.pallas_call(kernel, out_shape=(jax.ShapeDtypeStruct((width, hidden), f...  71.5 us
    unnamed x7, local copies, waits for them, and re-layouts  2.03 us
    broadcast_in_dim x2, other arithmetic, fused(): rows.transpose(1, 0, 2)[None]  1.89 us

profile of v7, /device:TPU:0, one launch (start us, length us, event | category | flops | bytes accessed | tf_op | source)
XLA Modules:
  0.0 76.1 jit_solution(13999399007756122016)
XLA Ops:
  0.6 0.0 copy-start
  0.6 0.0 copy-start.1
  0.7 0.0 copy-start.2
  0.7 71.5 %shard_map.120 = (f32[512,2048]{1,0:T(8,128)S(1)}, f32[12,4,1024]{2,1,0:T(4,128)S(1)}, f32[12,4,1024]{2,1,0:T(4,128)S(1)}) custom-call(bf16[2,512,512]{2,1,0:T(8,128)(2,1)} %emb_hbm.1, bf16[2,512,512]{2,1,0:T(8,128)(2,1)} %resid_hbm.1, bf16[2,64,2048]{2,1,0:T(8,128)(2,1)} %qg_hbm.1, bf16[512,2048]{1,0:T(8,128)(2,1)} %w_hbm.1, s32[2,4,512]{2,1,0:T(4,128)} %bitcast.43, ...), custom_call_target="tpu_custom_call" | custom-call | flops 3000000000 | bytes 20000000 | tf_op jit(solution)/shard_map/pallas_call | solution.py:519
  72.1 0.0 copy-done
  72.2 0.8 %fusion.2 = (f32[1,4,12,1024]{3,1,2,0:T(4,128)}, pred[12,4,1024]{2,1,0:T(4,128)(4,1)S(1)}) fusion(f32[1,4,12,1024]{3,1,2,0:T(4,128)S(1)} %copy-done, f32[12,4,1024]{2,1,0:T(4,128)S(1)} %get-tuple-element.9, f32[12,4,1024]{2,1,0:T(4,128)S(1)} %get-tuple-element.8), kind=kLoop, calls=%fused_computation.6 | loop fusion | flops 294912 | bytes 835584 | tf_op jit(solution)/shard_map/broadcast_in_dim | solution.py:576
  73.0 0.0 copy-done.1
  73.0 0.0 copy-done.2
  73.0 1.1 %fusion.4 = (f32[1,4,12,1024]{3,1,2,0:T(4,128)}, f32[1,4,12,1024]{3,1,2,0:T(4,128)}) fusion(pred[12,4,1024]{2,1,0:T(4,128)(4,1)S(1)} %get-tuple-element.11, f32[1,4,12,1024]{3,1,2,0:T(4,128)S(1)} %copy-done.1, f32[12,4,1024]{2,1,0:T(4,128)S(1)} %get-tuple-element.9, f32[1,4,12,1024]{3,1,2,0:T(4,128)S(1)} %copy-done, f32[1,4,12,1024]{3,1,2,0:T(4,128)S(1)} %copy-done.2), kind=kLoop, calls=%fused_computation.10 | loop fusion | flops 688128 | bytes 1228800 | tf_op jit(solution)/shard_map/broadcast_in_dim | solution.py:576
  74.0 2.0 %copy.14 = f32[512,2048]{1,0:T(8,128)} copy(f32[512,2048]{1,0:T(8,128)S(1)} %get-tuple-element.18) | data formatting | bytes 8388608
Async XLA Ops:
  0.6 71.5 %copy-start = (f32[1,4,12,1024]{3,1,2,0:T(4,128)S(1)}, f32[1,4,12,1024]{3,1,2,0:T(4,128)}, u32[]{:S(2)}) copy-start(f32[1,4,12,1024]{3,1,2,0:T(4,128)} %param.17) | copy-start | bytes 589828
  0.6 72.3 %copy-start.1 = (f32[1,4,12,1024]{3,1,2,0:T(4,128)S(1)}, f32[1,4,12,1024]{3,1,2,0:T(4,128)}, u32[]{:S(2)}) copy-start(f32[1,4,12,1024]{3,1,2,0:T(4,128)} %param.16) | copy-start | bytes 589828
  0.7 72.3 %copy-start.2 = (f32[1,4,12,1024]{3,1,2,0:T(4,128)S(1)}, f32[1,4,12,1024]{3,1,2,0:T(4,128)}, u32[]{:S(2)}) copy-start(f32[1,4,12,1024]{3,1,2,0:T(4,128)} %param.15) | copy-start | bytes 589828

commit v8 on v6

--- a/solution.py
+++ b/solution.py
@@ -127,11 +127,18 @@
     w,
     gq,
     prod,
-    part_recv,
+    p_send,
+    p_recv,
+    ps_send,
+    ps_recv,
     q_send,
     q_recv,
     s_send,
     s_recv,
+    f_send,
+    f_recv,
+    fs_send,
+    fs_recv,
     res,
     bucket,
     b_send,
@@ -145,9 +152,11 @@
     g_send_sem,
     g_recv_sem,
     p_sem,
+    ps_sem,
     q_sem,
     s_sem,
     f_sem,
+    fs_sem,
     o_sem,
     b_sem,
     y_sem,
@@ -275,8 +284,11 @@
             src_ref=src, dst_ref=dst, send_sem=sems.at[0], recv_sem=sems.at[1], device_id=(ynb, me), device_id_type=MESH
         )
 
-    def part_copy(c):
-        return sibling_copy(prod.at[c, 0:rows], part_recv.at[c], p_sem.at[c])
+    def part_copies(c):
+        return sibling_copy(p_send.at[c], p_recv.at[c], p_sem.at[c]), sibling_copy(ps_send.at[c], ps_recv.at[c], ps_sem.at[c])
+
+    def final_copies(c):
+        return sibling_copy(f_send.at[c], f_recv.at[c], f_sem.at[c]), sibling_copy(fs_send.at[c], fs_recv.at[c], fs_sem.at[c])
 
     def q_copy(c):
         return y_copy(q_send.at[c], q_recv.at[c], q_sem.at[c])
@@ -287,11 +299,17 @@
     def out_rows(k):
         return pl.ds(pl.multiple_of(k * rows, rows), rows)
 
-    def final_copy(c):
-        return sibling_copy(res.at[c], out_hbm.at[out_rows(core), span(c)], f_sem.at[c])
-
-    def out_copy(c):
-        return pltpu.make_async_copy(res.at[c], out_hbm.at[out_rows(core), span(c)], o_sem.at[c])
+    def out_copy(c, k):
+        half_rows = out_rows(core if k == 0 else 1 - core)
+        return pltpu.make_async_copy(res.at[c, k], out_hbm.at[half_rows, span(c)], o_sem.at[c, k])
+
+    def encode(total, codes, scales):
+        top = jnp.maximum(jnp.max(jnp.abs(total), axis=0, keepdims=True), 1e-30)
+        codes[...] = jnp.round(total * (32767.0 / top)).astype(jnp.int32).astype(jnp.int16)
+        scales[...] = jnp.broadcast_to(top * (1.0 / 32767.0), scales.shape)
+
+    def decode(codes, scales):
+        return codes[...].astype(jnp.int32).astype(jnp.float32) * scales[0:1, :]
 
     def dot(a, b):
         return jnp.dot(a, b, preferred_element_type=jnp.float32)
@@ -311,7 +329,9 @@
         own_load(c).wait()
         block = gq[c].reshape(micro * mine * 8, cols)
         prod[c] = dot(left[...], block)
-        part_copy(c).start()
+        encode(prod[c, 0:rows, :], p_send.at[c], ps_send.at[c])
+        for copy in part_copies(c):
+            copy.start()
         sums = prod[c, width:, :]
         high = sums.astype(jnp.bfloat16)
         low = (sums - high.astype(jnp.float32)).astype(jnp.bfloat16)
@@ -320,23 +340,30 @@
         bucket[...] += terms[0:slots] + terms[slots : 2 * slots]
 
     def core_sum(c):
-        part_copy(c).wait_recv()
-        total = prod[c, rows:width, :] + part_recv[c]
-        top = jnp.maximum(jnp.max(jnp.abs(total), axis=0, keepdims=True), 1e-30)
-        codes = jnp.round(total * (32767.0 / top))
-        q_send[c] = codes.astype(jnp.int32).astype(jnp.int16)
-        s_send[c] = jnp.broadcast_to(top * (1.0 / 32767.0), s_send.shape[1:])
+        for copy in part_copies(c):
+            copy.wait_recv()
+        total = prod[c, rows:width, :] + decode(p_recv.at[c], ps_recv.at[c])
+        encode(total, q_send.at[c], s_send.at[c])
         q_copy(c).start()
         s_copy(c).start()
 
     def finish(c):
         q_copy(c).wait_recv()
         s_copy(c).wait_recv()
-        here = q_send[c].astype(jnp.int32).astype(jnp.float32) * s_send[c][0:1, :]
-        there = q_recv[c].astype(jnp.int32).astype(jnp.float32) * s_recv[c][0:1, :]
-        res[c] = jnp.where(y == 0, here, there) + jnp.where(y == 0, there, here)
-        final_copy(c).start()
-        out_copy(c).start()
+        here = decode(q_send.at[c], s_send.at[c])
+        there = decode(q_recv.at[c], s_recv.at[c])
+        total = jnp.where(y == 0, here, there) + jnp.where(y == 0, there, here)
+        encode(total, f_send.at[c], fs_send.at[c])
+        for copy in final_copies(c):
+            copy.start()
+        res[c, 0] = decode(f_send.at[c], fs_send.at[c])
+        out_copy(c, 0).start()
+
+    def take(c):
+        for copy in final_copies(c):
+            copy.wait_recv()
+        res[c, 1] = decode(f_recv.at[c], fs_recv.at[c])
+        out_copy(c, 1).start()
 
     def guarded(c, stage):
         @pl.when((c >= 0) & (c < CHUNKS))
@@ -395,11 +422,10 @@
         for far in (1, 2, 3):
             each_forward(c, far, sent, False)
         each_relay(c, sent, False)
-        part_copy(c).wait_send()
-        q_copy(c).wait_send()
-        s_copy(c).wait_send()
-        final_copy(c).wait()
-        out_copy(c).wait()
+        for copy in (*part_copies(c), q_copy(c), s_copy(c), *final_copies(c)):
+            copy.wait_send()
+        for k in range(2):
+            out_copy(c, k).wait()
 
     def slot(s, carry):
         guarded(s + LEAD - 1, lambda c: each_own(c, start))
@@ -409,7 +435,8 @@
         guarded(s - 4, compute)
         guarded(s - 5, core_sum)
         guarded(s - 7, finish)
-        guarded(s - 8, drain)
+        guarded(s - 8, take)
+        guarded(s - 9, drain)
         return carry
 
     lax.fori_loop(1, CHUNKS + 3, slot, 0)
@@ -437,8 +464,10 @@
     rows_copy.start()
     core_sum(CHUNKS - 1)
     finish(CHUNKS - 4)
-    drain_some(CHUNKS - 5, CHUNKS - 4)
+    take(CHUNKS - 5)
+    drain_some(CHUNKS - 6, CHUNKS - 5)
     finish(CHUNKS - 3)
+    take(CHUNKS - 4)
     rows_copy.wait_recv()
     a_send[...] = y_send[...] + y_recv[...]
 
@@ -468,13 +497,15 @@
         a_copy(step).start()
     a_recv[me] = a_send[pl.ds(pl.multiple_of(me * SLOT, SLOT), SLOT), :]
     finish(CHUNKS - 2)
-    drain_some(CHUNKS - 4, CHUNKS - 3)
+    take(CHUNKS - 3)
+    drain_some(CHUNKS - 5, CHUNKS - 3)
     for step in range(1, 8):
         a_arrived(step).wait_recv()
     h_copy = sibling_copy(a_recv, sib_recv, h_sem)
     h_copy.start()
     finish(CHUNKS - 1)
-    drain_some(CHUNKS - 3, CHUNKS - 1)
+    take(CHUNKS - 2)
+    drain_some(CHUNKS - 3, CHUNKS - 2)
     h_copy.wait_recv()
     for t in range(8):
         for k in range(2):
@@ -488,7 +519,8 @@
     for step in range(1, 8):
         a_copy(step).wait_send()
 
-    drain_some(CHUNKS - 1, CHUNKS)
+    take(CHUNKS - 1)
+    drain_some(CHUNKS - 2, CHUNKS)
 
 
 def fused(
@@ -535,12 +567,13 @@
             vmem((width, hidden), bf16),
             vmem((CHUNKS, micro, group, cols), bf16),
             vmem((CHUNKS, width + slots, cols), f32),
-            vmem((CHUNKS, rows, cols), f32),
-            vmem((CHUNKS, rows, cols), i16),
-            vmem((CHUNKS, rows, cols), i16),
-            vmem((CHUNKS, 8, cols), f32),
-            vmem((CHUNKS, 8, cols), f32),
-            vmem((CHUNKS, rows, cols), f32),
+            *[vmem((CHUNKS, rows, cols), i16), vmem((CHUNKS, rows, cols), i16)],
+            *[vmem((CHUNKS, 8, cols), f32), vmem((CHUNKS, 8, cols), f32)],
+            *[vmem((CHUNKS, rows, cols), i16), vmem((CHUNKS, rows, cols), i16)],
+            *[vmem((CHUNKS, 8, cols), f32), vmem((CHUNKS, 8, cols), f32)],
+            *[vmem((CHUNKS, rows, cols), i16), vmem((CHUNKS, rows, cols), i16)],
+            *[vmem((CHUNKS, 8, cols), f32), vmem((CHUNKS, 8, cols), f32)],
+            vmem((CHUNKS, 2, rows, cols), f32),
             vmem((slots, width), f32),
             vmem((slots, half), f32),
             vmem((slots, half), f32),
@@ -552,11 +585,7 @@
             dma((5 + CHUNKS,)),
             dma((CHUNKS, tables, 3)),
             dma((CHUNKS, tables)),
-            dma((CHUNKS, 2)),
-            dma((CHUNKS, 2)),
-            dma((CHUNKS, 2)),
-            dma((CHUNKS, 2)),
-            dma((CHUNKS,)),
+            *[dma((CHUNKS, 2)) for _ in range(7)],
             dma((2,)),
             dma((2,)),
             dma((tables,)),

time: 74.5 us -> 74.9 us (level)
  no operation moved by 1% of the time
where the time goes in v8:
time: 74.9 us; the launch traced here: 74.7 us
  Pallas kernels  70.1 us (94%)
  local copies, waits for them, and re-layouts  2.03 us (3%)
  other arithmetic  1.89 us (3%)
    pallas_call x1, Pallas kernels, fused(): pl.pallas_call(kernel, out_shape=(jax.ShapeDtypeStruct((width, hidden), f...  70.1 us
    unnamed x7, local copies, waits for them, and re-layouts  2.03 us
    broadcast_in_dim x2, other arithmetic, fused(): rows.transpose(1, 0, 2)[None]  1.89 us

profile of v8, /device:TPU:0, one launch (start us, length us, event | category | flops | bytes accessed | tf_op | source)
XLA Modules:
  0.0 74.7 jit_solution(8618832636869576017)
XLA Ops:
  0.6 0.0 copy-start
  0.6 0.0 copy-start.1
  0.7 0.0 copy-start.2
  0.7 70.1 %shard_map.120 = (f32[512,2048]{1,0:T(8,128)S(1)}, f32[12,4,1024]{2,1,0:T(4,128)S(1)}, f32[12,4,1024]{2,1,0:T(4,128)S(1)}) custom-call(bf16[2,512,512]{2,1,0:T(8,128)(2,1)} %emb_hbm.1, bf16[2,512,512]{2,1,0:T(8,128)(2,1)} %resid_hbm.1, bf16[2,64,2048]{2,1,0:T(8,128)(2,1)} %qg_hbm.1, bf16[512,2048]{1,0:T(8,128)(2,1)} %w_hbm.1, s32[2,4,512]{2,1,0:T(4,128)} %bitcast.43, ...), custom_call_target="tpu_custom_call" | custom-call | flops 3000000000 | bytes 20000000 | tf_op jit(solution)/shard_map/pallas_call | solution.py:551
  70.8 0.0 copy-done
  70.8 0.8 %fusion.2 = (f32[1,4,12,1024]{3,1,2,0:T(4,128)}, pred[12,4,1024]{2,1,0:T(4,128)(4,1)S(1)}) fusion(f32[1,4,12,1024]{3,1,2,0:T(4,128)S(1)} %copy-done, f32[12,4,1024]{2,1,0:T(4,128)S(1)} %get-tuple-element.9, f32[12,4,1024]{2,1,0:T(4,128)S(1)} %get-tuple-element.8), kind=kLoop, calls=%fused_computation.6 | loop fusion | flops 294912 | bytes 835584 | tf_op jit(solution)/shard_map/broadcast_in_dim | solution.py:605
  71.6 0.0 copy-done.1
  71.6 0.0 copy-done.2
  71.6 1.1 %fusion.4 = (f32[1,4,12,1024]{3,1,2,0:T(4,128)}, f32[1,4,12,1024]{3,1,2,0:T(4,128)}) fusion(pred[12,4,1024]{2,1,0:T(4,128)(4,1)S(1)} %get-tuple-element.11, f32[1,4,12,1024]{3,1,2,0:T(4,128)S(1)} %copy-done.1, f32[12,4,1024]{2,1,0:T(4,128)S(1)} %get-tuple-element.9, f32[1,4,12,1024]{3,1,2,0:T(4,128)S(1)} %copy-done, f32[1,4,12,1024]{3,1,2,0:T(4,128)S(1)} %copy-done.2), kind=kLoop, calls=%fused_computation.10 | loop fusion | flops 688128 | bytes 1228800 | tf_op jit(solution)/shard_map/broadcast_in_dim | solution.py:605
  72.7 2.0 %copy.14 = f32[512,2048]{1,0:T(8,128)} copy(f32[512,2048]{1,0:T(8,128)S(1)} %get-tuple-element.18) | data formatting | bytes 8388608
Async XLA Ops:
  0.6 70.1 %copy-start = (f32[1,4,12,1024]{3,1,2,0:T(4,128)S(1)}, f32[1,4,12,1024]{3,1,2,0:T(4,128)}, u32[]{:S(2)}) copy-start(f32[1,4,12,1024]{3,1,2,0:T(4,128)} %param.17) | copy-start | bytes 589828
  0.6 71.0 %copy-start.1 = (f32[1,4,12,1024]{3,1,2,0:T(4,128)S(1)}, f32[1,4,12,1024]{3,1,2,0:T(4,128)}, u32[]{:S(2)}) copy-start(f32[1,4,12,1024]{3,1,2,0:T(4,128)} %param.16) | copy-start | bytes 589828
  0.7 71.0 %copy-start.2 = (f32[1,4,12,1024]{3,1,2,0:T(4,128)S(1)}, f32[1,4,12,1024]{3,1,2,0:T(4,128)}, u32[]{:S(2)}) copy-start(f32[1,4,12,1024]{3,1,2,0:T(4,128)} %param.15) | copy-start | bytes 589828

commit v9 on v6

--- a/solution.py
+++ b/solution.py
@@ -102,7 +102,7 @@
 
 
 LEAD = 3
-CHUNKS = 8
+CHUNKS = 4
 SLOT = 16
 MESH = pl.DeviceIdType.MESH
 UP, DOWN, ACROSS = 0, 1, 2
@@ -419,7 +419,7 @@
             drain(c)
             return carry
 
-        lax.fori_loop(low, high, one, 0)
+        lax.fori_loop(max(low, 0), high, one, 0)
 
     half = b_send.shape[1]
 

time: 74.5 us -> 81.3 us (1.091)
  Pallas kernels: 69.8 us -> 76.6 us
    pallas_call x1, Pallas kernels: 69.8 us -> 76.6 us  [fused(): pl.pallas_call(kernel, out_shape=(jax.ShapeDtypeStruct((width, hidden), f...]
where the time goes in v9:
time: 81.3 us; the launch traced here: 81.1 us
  Pallas kernels  76.6 us (94%)
  local copies, waits for them, and re-layouts  2.03 us (2%)
  other arithmetic  1.89 us (2%)
    pallas_call x1, Pallas kernels, fused(): pl.pallas_call(kernel, out_shape=(jax.ShapeDtypeStruct((width, hidden), f...  76.6 us
    unnamed x7, local copies, waits for them, and re-layouts  2.03 us
    broadcast_in_dim x2, other arithmetic, fused(): rows.transpose(1, 0, 2)[None]  1.89 us

profile of v9, /device:TPU:0, one launch (start us, length us, event | category | flops | bytes accessed | tf_op | source)
XLA Modules:
  0.0 81.1 jit_solution(5804166932284055691)
XLA Ops:
  0.6 0.0 copy-start
  0.6 0.0 copy-start.1
  0.7 0.0 copy-start.2
  0.7 76.6 %shard_map.120 = (f32[512,2048]{1,0:T(8,128)S(1)}, f32[12,4,1024]{2,1,0:T(4,128)S(1)}, f32[12,4,1024]{2,1,0:T(4,128)S(1)}) custom-call(bf16[2,512,512]{2,1,0:T(8,128)(2,1)} %emb_hbm.1, bf16[2,512,512]{2,1,0:T(8,128)(2,1)} %resid_hbm.1, bf16[2,64,2048]{2,1,0:T(8,128)(2,1)} %qg_hbm.1, bf16[512,2048]{1,0:T(8,128)(2,1)} %w_hbm.1, s32[2,4,512]{2,1,0:T(4,128)} %bitcast.43, ...), custom_call_target="tpu_custom_call" | custom-call | flops 3000000000 | bytes 20000000 | tf_op jit(solution)/shard_map/pallas_call | solution.py:519
  77.2 0.0 copy-done
  77.2 0.8 %fusion.2 = (f32[1,4,12,1024]{3,1,2,0:T(4,128)}, pred[12,4,1024]{2,1,0:T(4,128)(4,1)S(1)}) fusion(f32[1,4,12,1024]{3,1,2,0:T(4,128)S(1)} %copy-done, f32[12,4,1024]{2,1,0:T(4,128)S(1)} %get-tuple-element.9, f32[12,4,1024]{2,1,0:T(4,128)S(1)} %get-tuple-element.8), kind=kLoop, calls=%fused_computation.6 | loop fusion | flops 294912 | bytes 835584 | tf_op jit(solution)/shard_map/broadcast_in_dim | solution.py:576
  78.1 0.0 copy-done.1
  78.1 0.0 copy-done.2
  78.1 1.1 %fusion.4 = (f32[1,4,12,1024]{3,1,2,0:T(4,128)}, f32[1,4,12,1024]{3,1,2,0:T(4,128)}) fusion(pred[12,4,1024]{2,1,0:T(4,128)(4,1)S(1)} %get-tuple-element.11, f32[1,4,12,1024]{3,1,2,0:T(4,128)S(1)} %copy-done.1, f32[12,4,1024]{2,1,0:T(4,128)S(1)} %get-tuple-element.9, f32[1,4,12,1024]{3,1,2,0:T(4,128)S(1)} %copy-done, f32[1,4,12,1024]{3,1,2,0:T(4,128)S(1)} %copy-done.2), kind=kLoop, calls=%fused_computation.10 | loop fusion | flops 688128 | bytes 1228800 | tf_op jit(solution)/shard_map/broadcast_in_dim | solution.py:576
  79.1 2.0 %copy.14 = f32[512,2048]{1,0:T(8,128)} copy(f32[512,2048]{1,0:T(8,128)S(1)} %get-tuple-element.18) | data formatting | bytes 8388608
Async XLA Ops:
  0.6 76.6 %copy-start = (f32[1,4,12,1024]{3,1,2,0:T(4,128)S(1)}, f32[1,4,12,1024]{3,1,2,0:T(4,128)}, u32[]{:S(2)}) copy-start(f32[1,4,12,1024]{3,1,2,0:T(4,128)} %param.17) | copy-start | bytes 589828
  0.6 77.4 %copy-start.1 = (f32[1,4,12,1024]{3,1,2,0:T(4,128)S(1)}, f32[1,4,12,1024]{3,1,2,0:T(4,128)}, u32[]{:S(2)}) copy-start(f32[1,4,12,1024]{3,1,2,0:T(4,128)} %param.16) | copy-start | bytes 589828
  0.7 77.4 %copy-start.2 = (f32[1,4,12,1024]{3,1,2,0:T(4,128)S(1)}, f32[1,4,12,1024]{3,1,2,0:T(4,128)}, u32[]{:S(2)}) copy-start(f32[1,4,12,1024]{3,1,2,0:T(4,128)} %param.15) | copy-start | bytes 589828
